TPU v7x, 256 devices: a whole 4x4x8 slice. The times are simulated.
256 devices in a mesh: row: 8 (over y, core), col: 8 (over z), shot: 4 (over x).
Axes of the slice: x: 4, y: 4, z: 8, core: 2. Of those that a mesh axis runs over, the one named last changes fastest.
Arguments:
- right_side: float32 [256, 16, 512], P('shot', None, 'col'), may hold values from -6 to 6
- rest_solution: bfloat16 [256, 64, 512], P('shot', 'row', 'col'), may hold values from -6 to 6
- rest_basis: bfloat16 [64, 1024, 512], P('row'), may hold values from -0.25 to 0.25
- window_basis: bfloat16 [64, 64, 16, 512], P('row', None, None, 'col'), may hold values from -0.125 to 0.125
- ranks: int32 [64, 16], P('row'), may hold values from 1 to 64, as said below
- inverses: bfloat16 [16, 512, 512], P(None, ('row', 'col')), may hold values from -0.25 to 0.25
- child_map: int32 [2, 4096], replicated, may hold values from 0 to 8191, as said below
Outputs:
- solution: bfloat16 [256, 16, 512], P('shot', None, ('row', 'col'))
- child_values: bfloat16 [256, 2, 4096], P('shot', None, ('row', 'col'))
Inputs may be any that keep to these rules, and one draw needn't show every extreme that they name: `ranks`: each tile's rank lies in 1 to 64, and some tile has rank 64. `child_map`: a window row index i * 512 + p; every window row is taken exactly once over both children. With G = 8 * 8 grid devices, grid device g = row index * 8 + col index holds the positions p with p // (512 // G) == g and the child rows q with q // (4096 // G) == g of each child; the child rows that device g holds take, from any one grid device, either none or exactly 4 window rows.
All inputs are finite; a program needn't handle non-finite values.
Results may differ from a plain program's by a relative error of at most 0.018.
Values may be sent and summed in bfloat16 or wider, within the bound.
A program may use at most 64 MiB of HBM per device.

v0:
```python
import jax
import jax.numpy as jnp
from jax import lax
from jax.sharding import PartitionSpec as P


def on_device(right_side, rest_solution, rest_basis, window_basis, ranks, inverses, child_map):
    sources = right_side.shape[0]
    tiles_here = rest_basis.shape[0]
    window_tiles = right_side.shape[1]
    rank_width = window_basis.shape[1]
    coeffs = jnp.einsum(
        "jap,sjp->jas",
        rest_basis,
        lax.all_gather(rest_solution, "col", axis=2, tiled=True),
        preferred_element_type=jnp.float32,
    )
    coeffs = coeffs.reshape(tiles_here, window_tiles, rank_width, sources)
    rank_mask = jnp.arange(rank_width, dtype=jnp.int32)[None, None, :] < ranks[:, :, None]
    masked = jnp.where(rank_mask[..., None], coeffs, jnp.float32(0.0)).astype(jnp.bfloat16)
    partial_update = jnp.einsum(
        "jkip,jiks->sip", window_basis, masked, preferred_element_type=jnp.float32
    )
    update = lax.psum(partial_update.astype(jnp.bfloat16), "row").astype(jnp.float32)
    reduced = (right_side - update).astype(jnp.bfloat16)
    solved = jnp.einsum(
        "ipm,sim->sip",
        inverses,
        lax.all_gather(reduced, "col", axis=2, tiled=True),
        preferred_element_type=jnp.float32,
    )
    solution = solved.astype(jnp.bfloat16)
    grid_count = lax.axis_size("row") * lax.axis_size("col")
    grid_index = lax.axis_index("row") * lax.axis_size("col") + lax.axis_index("col")
    child_count = child_map.shape[1] // grid_count
    tile_length = inverses.shape[2]
    gathered_rows = lax.all_gather(solution, ("row", "col"), axis=2, tiled=True)
    own_map = lax.dynamic_slice_in_dim(child_map, grid_index * child_count, child_count, 1)
    flat_rows = gathered_rows.reshape(sources, window_tiles * tile_length)
    child_values = flat_rows[:, own_map]
    return (solution, child_values)


def solution(mesh):
    in_specs = (
        P("shot", None, "col"),
        P("shot", "row", "col"),
        P("row", None, None),
        P("row", None, None, "col"),
        P("row", None),
        P(None, ("row", "col"), None),
        P(),
    )
    out_specs = (P("shot", None, ("row", "col")), P("shot", None, ("row", "col")))
    return jax.shard_map(
        on_device, mesh=mesh, in_specs=in_specs, out_specs=out_specs, check_vma=False
    )
```

profile of v0, /device:TPU:1, one launch (start us, length us, event | category | flops | bytes accessed | tf_op | source)
XLA Modules:
  0.0 244.3 jit_solution(15362249334024237251)
XLA Ops:
  7.2 0.0 copy-start
  7.2 0.0 all-reduce.2.cloned.1.call-start
  7.2 1.2 copy.12
  8.4 25.7 %all_gather.9 = bf16[64,8,512]{0,1,2:T(8,128)(2,1)S(1)} all-gather(bf16[64,8,64]{0,1,2:T(8,128)(2,1)S(1)} %copy.12), channel_id=1, replica_groups=mesh['row'=8,'col'=8,'shot'=4] {'col'}, dimensions={2}, use_global_device_ids=true | all-gather | bytes 589824 | tf_op jit(solution)/shard_map/all_gather | solution.py:15
  34.1 6.0 %fusion.11 = bf16[8,1024,64]{1,2,0:T(8,128)(2,1)S(1)} fusion(bf16[8,1024,512]{2,1,0:T(8,128)(2,1)} %param.9, bf16[64,8,512]{0,1,2:T(8,128)(2,1)S(1)} %all_gather.9), kind=kOutput, calls=%fused_computation.9 | convolution fusion | flops 536870912 | bytes 9961472 | tf_op jit(solution)/shard_map/jap,sjp->jas/dot_general | solution.py:12
  40.1 0.0 copy-start.2
  40.1 2.4 reshape.14
  42.5 0.0 copy-done.2
  42.5 0.1 iota_compare_fusion
  42.6 2.1 select_convert_fusion
  44.7 0.0 copy-done
  44.7 0.0 copy-start.1
  44.7 1.7 fusion
  46.4 0.0 copy-start.3
  46.4 0.3 copy.19
  46.6 0.7 fusion.13
  47.4 0.0 all-reduce.2.cloned.1.call-update
  47.4 0.0 all-gather.3.cloned.1.call-start
  47.4 0.0 copy-done.1
  47.4 0.4 copy.14
  47.8 67.6 %all-reduce.2.cloned.1.call-done = bf16[64,16,64]{0,1,2:T(8,128)(2,1)} async-done(((bf16[64,16,64]{0,1,2:T(8,128)(2,1)}), bf16[64,16,64]{0,1,2:T(8,128)(2,1)}) %all-reduce.2.cloned.1.call-update) | async-done | bytes 131088 | tf_op jit(solution)/shard_map/psum | solution.py:24
  115.4 1.7 subtract_convert_fusion
  117.1 0.0 all-gather.3.cloned.1.call-update
  117.1 0.0 all-gather.5.cloned.1.call-start
  117.2 38.8 %all-gather.3.cloned.1.call-done = bf16[64,16,512]{0,1,2:T(8,128)(2,1)} async-done(((bf16[64,16,64]{0,1,2:T(8,128)(2,1)}), bf16[64,16,512]{0,1,2:T(8,128)(2,1)}) %all-gather.3.cloned.1.call-update) | async-done | bytes 1048592 | tf_op jit(solution)/shard_map/all_gather | solution.py:29
  156.0 0.0 copy-done.3
  156.0 2.9 %fusion.8 = bf16[64,16,8]{0,2,1:T(8,128)(2,1)} fusion(bf16[16,8,512]{2,1,0:T(8,128)(2,1)S(1)} %copy-done.3, bf16[64,16,512]{0,1,2:T(8,128)(2,1)} %all-gather.3.cloned.1.call-done), kind=kOutput, calls=%fused_computation.8 | convolution fusion | flops 8396800 | bytes 1196032 | tf_op jit(solution)/shard_map/ipm,sim->sip/dot_general | solution.py:26
  158.9 0.0 all-gather.5.cloned.1.call-update
  158.9 0.8 compare_select_fusion
  159.7 0.1 reshape.18
  159.8 74.8 %all-gather.5.cloned.1.call-done = bf16[64,16,512]{0,2,1:T(8,128)(2,1)} async-done(((bf16[64,16,8]{0,2,1:T(8,128)(2,1)}), bf16[64,16,512]{0,2,1:T(8,128)(2,1)}) %all-gather.5.cloned.1.call-update) | async-done | bytes 1048592 | tf_op jit(solution)/shard_map/all_gather | solution.py:37
  234.6 2.5 %gather_fusion = bf16[128,64]{1,0:T(8,128)(2,1)S(1)} fusion(bf16[64,8192]{0,1:T(8,128)(2,1)} %bitcast.16, s32[1024]{0:T(1024)S(1)} %pad_clamp_fusion), kind=kCustom, calls=%fused_computation | custom fusion | bytes 33280 | tf_op jit(solution)/shard_map/gather | solution.py:40
  237.1 0.7 copy.16
  (1 shorter events, 0.0 us)
Async XLA Ops:
  7.2 37.5 %copy-start = (bf16[8,64,16,64]{3,2,1,0:T(8,128)(2,1)S(1)}, bf16[8,64,16,64]{3,2,1,0:T(8,128)(2,1)}, u32[]{:S(2)}) copy-start(bf16[8,64,16,64]{3,2,1,0:T(8,128)(2,1)} %param.10) | copy-start | bytes 3145732
  7.2 108.2 %all-reduce.2.cloned.1.call-start = ((), (), s32[]{:S(2)}) async-start(), calls=%async_computation | async-start | bytes 524288 | tf_op jit(solution)/shard_map/psum | solution.py:24
  40.1 2.4 copy-start.2
  44.7 2.8 %copy-start.1 = (f32[64,16,64]{2,1,0:T(8,128)S(1)}, f32[64,16,64]{2,1,0:T(8,128)}, u32[]{:S(2)}) copy-start(f32[64,16,64]{2,1,0:T(8,128)} %param.7) | copy-start | bytes 786436
  46.4 109.6 %copy-start.3 = (bf16[16,8,512]{2,1,0:T(8,128)(2,1)S(1)}, bf16[16,8,512]{2,1,0:T(8,128)(2,1)}, u32[]{:S(2)}) copy-start(bf16[16,8,512]{2,1,0:T(8,128)(2,1)} %param.12) | copy-start | bytes 393220
  47.4 108.6 %all-gather.3.cloned.1.call-start = ((), (), s32[]{:S(2)}) async-start(), calls=%async_computation.1 | async-start | bytes 2359296 | tf_op jit(solution)/shard_map/all_gather | solution.py:29
  117.1 117.4 %all-gather.5.cloned.1.call-start = ((), (), s32[]{:S(2)}) async-start(), calls=%async_computation.2 | async-start | bytes 2129920 | tf_op jit(solution)/shard_map/all_gather | solution.py:37
Sparse Core Ops, SparseCore 0:
  47.5 67.8 all-reduce.1
  117.3 38.5 all-gather.2
  159.4 75.1 all-gather.4
where the time goes:
time: 245 us; the launch traced here: 244 us
  waiting for transfers between devices  181 us (74%)
  blocking collectives  25.7 us (10%)
  between operations  13.8 us (6%)
  matrix products  10.6 us (4%)
  local copies, waits for them, and re-layouts  8.25 us (3%)
  other arithmetic  4.61 us (2%)
    all_gather x1, waiting for transfers between devices, on_device(): gathered_rows = lax.all_gather(solution, ('row', 'col'), axis=2, tiled=True)  74.8 us
    psum x1, waiting for transfers between devices, on_device(): lax.psum(partial_update.astype(jnp.bfloat16), 'row').astype(jnp.float32)  67.6 us
    all_gather x1, waiting for transfers between devices, on_device(): lax.all_gather(reduced, 'col', axis=2, tiled=True)  38.8 us
    all_gather x1, blocking collectives, on_device(): lax.all_gather(rest_solution, 'col', axis=2, tiled=True)  25.7 us
    dot_general x1, matrix products, on_device(): jnp.einsum('jap,sjp->jas', rest_basis, lax.all_gather(rest_solution, 'col...  6.04 us
  transfers between devices with their start and end apart: 3, of which 3 were waited for; matrix products, arithmetic and copies ran while one was open for 0% of the time, Pallas kernels for 0%

commit v1 on v0

v1 whole, which is shorter than its diff:
```python
import jax
import jax.numpy as jnp
from jax import lax
from jax.experimental import pallas as pl
from jax.experimental.pallas import tpu as pltpu
from jax.sharding import PartitionSpec as P

MESH = pl.DeviceIdType.MESH
F32 = jnp.float32
BF16 = jnp.bfloat16
I32 = jnp.int32
N = 8


def iota(shape, axis):
    return lax.broadcasted_iota(I32, shape, axis)


def dot(a, b):
    return jnp.dot(a, b, preferred_element_type=F32)


def dot_tn(a, b):
    return lax.dot_general(a, b, (((0,), (0,)), ((), ())), preferred_element_type=F32)


def swap(x):
    return pltpu.roll(x, 64, 1)


def kernel(
    right_ref, sol_ref, basis_ref, wb_ref, ranks_ref, inv_ref, map_ref,
    out_sol, out_child,
    sol_v, sol_f, right_v, right_f, basis_v, wb_v, map_v, ranks_s,
    gath, w0, cm, msg, part, red, redg, invg, invl, solg, selm, s5, pk, chg,
    load_sem, basis_sem, ring_send, ring_recv, inv_send, inv_recv,
    p2_send, p2_recv, p3_send, p3_recv, p4_send, p4_recv, p5_send, p5_recv,
):
    r = lax.axis_index("row")
    c = lax.axis_index("col")
    right, left = lax.rem(c + 1, N), lax.rem(c + N - 1, N)

    def remote(src, dst, send, recv, axis, to):
        return pltpu.make_async_remote_copy(
            src_ref=src, dst_ref=dst, send_sem=send, recv_sem=recv,
            device_id={axis: to}, device_id_type=MESH,
        )

    load_sol = pltpu.make_async_copy(sol_ref, sol_v, load_sem.at[0])
    load_sol.start()
    load_wb = pltpu.make_async_copy(wb_ref, wb_v, load_sem.at[1])
    load_map = pltpu.make_async_copy(
        map_ref.at[:, pl.ds(pl.multiple_of(r * 512, 512), 512)], map_v, load_sem.at[2])
    load_ranks = pltpu.make_async_copy(ranks_ref, ranks_s, load_sem.at[3])
    load_right = pltpu.make_async_copy(
        right_ref.at[:, pl.ds(pl.multiple_of((r // 4) * 8, 8), 8), :], right_v, load_sem.at[4])
    load_inv = pltpu.make_async_copy(
        inv_ref.at[pl.ds(2 * r, 2)], invg.at[r], load_sem.at[5])

    barrier = pltpu.get_barrier_semaphore()
    for d in range(1, N):
        pl.semaphore_signal(barrier, inc=1, device_id={"col": lax.rem(c + d, N)}, device_id_type=MESH)
        pl.semaphore_signal(barrier, inc=1, device_id={"row": lax.rem(r + d, N)}, device_id_type=MESH)

    load_wb.start()
    load_map.start()
    load_ranks.start()
    load_right.start()
    load_inv.start()
    loads = [
        pltpu.make_async_copy(basis_ref.at[j], basis_v.at[j], basis_sem.at[j])
        for j in range(N)
    ]
    for load in loads:
        load.start()

    load_sol.wait()
    sol_f[...] = sol_v[...].astype(F32).reshape(512, 64)
    for jj in range(4):
        both = jnp.concatenate(
            [sol_f[pl.ds(2 * jj + h, 64, stride=8), :] for h in range(2)], axis=0)
        gath[jj, c] = both.T.astype(BF16)

    pl.semaphore_wait(barrier, 2 * (N - 1))

    def hop(jj, slot, to, way, step):
        return remote(gath.at[jj, slot], gath.at[jj, slot],
                      ring_send.at[way, step, jj], ring_recv.at[way, step, jj], "col", to)

    def slot_of(way, step):
        return lax.rem(c + (N - step if way == 0 else step), N)

    def ring_hop(step):
        for jj in range(4):
            for way in range(2):
                if step > 0:
                    hop(jj, slot_of(way, step), right, way, step - 1).wait_recv()
                if step < 3 or jj % 2 == way:
                    hop(jj, slot_of(way, step), (right, left)[way], way, step).start()

    ring_hop(0)
    for d in range(1, N):
        to = lax.rem(r + d, N)
        remote(inv_ref.at[pl.ds(2 * to, 2)], invg.at[r], inv_send.at[d], inv_recv.at[d], "row", to).start()

    load_wb.wait()
    row_i, col_i = iota((256, 256), 0), iota((256, 256), 1)
    perm = jnp.where(
        ((row_i >> 4) == (col_i & 15)) & ((row_i & 15) == (col_i >> 4)), 1.0, 0.0).astype(BF16)

    def regroup(step):
        jj, kb = step // 4, step % 4
        k0 = pl.multiple_of(kb * 16, 16)
        x = jnp.concatenate(
            [wb_v[2 * jj + h, pl.ds(k0, 16)].reshape(256, 64) for h in range(2)], axis=1)
        y = dot(perm, x).astype(BF16).reshape(16, 16, 128)
        w0[:, pl.ds(pl.multiple_of(jj * 64 + kb * 16, 16), 16), :] = y

    for step in range(8):
        regroup(step)
    ring_hop(1)
    for step in range(8, 16):
        regroup(step)
    ring_hop(2)

    low = iota((1, 128), 1) < 64
    load_map.wait()
    w = map_v[...]
    cc = (w >> 3) & 7
    code = (((w >> 9) & 1) << 9) + ((w >> 10) << 6) + (((w >> 6) & 7) << 3) + (w & 7) + 1
    mine = cc == c
    mine_f = jnp.where(mine, 1.0, 0.0)
    mine8 = jnp.where(iota((8, 512), 0) == 0, mine_f[0:1], mine_f[1:2]).astype(BF16)
    ta, tb = iota((512, 512), 0), iota((512, 512), 1)
    same = (ta >> 6) == (tb >> 6)
    before = dot(mine8, jnp.where(same & (ta < tb), 1.0, 0.0).astype(BF16))
    total = dot(mine8, jnp.where(same, 1.0, 0.0).astype(BF16))
    place = (before[0:1].astype(I32), (before[1:2] + total[0:1]).astype(I32))
    code_f = jnp.where(mine, code, 0).astype(F32)
    slots = []
    for g in range(4):
        at = slice(g * 128, (g + 1) * 128)
        ra, la = iota((64, 128), 0), iota((64, 128), 1)
        ours = (ra >> 5) == (la >> 6)
        acc = jnp.zeros((64, 128), F32)
        for ch in range(2):
            take = ours & ((ra & 31) == place[ch][:, at])
            acc = acc + jnp.where(take, code_f[ch:ch + 1, at], 0.0)
        slots.append(jnp.sum(acc, axis=1, keepdims=True))
    slot = jnp.concatenate(slots, axis=0).astype(I32)
    src = iota((256, 512), 1) + 1
    for h in range(2):
        selm[h * 256:(h + 1) * 256, :] = jnp.where(src + h * 512 == slot, 1.0, 0.0).astype(BF16)
    ra, la = iota((64, 512), 0), iota((64, 512), 1)
    selm[512:576, :] = jnp.where(
        la == ((ra >> 3) << 6) + r * 8 + (ra & 7), 1.0, 0.0).astype(BF16)

    x = map_v[:, pl.ds(pl.multiple_of((c // 2) * 128, 128), 128)]
    x_swapped = swap(x)
    odd = lax.rem(c, 2) == 1
    own = jnp.where(
        low, jnp.where(odd, x_swapped[0:1], x[0:1]), jnp.where(odd, x[1:2], x_swapped[1:2]))
    class_l = ((own >> 3) & 7).astype(F32)
    qa, qb = iota((128, 128), 0), iota((128, 128), 1)
    class_s = jnp.sum(jnp.where(qa == qb, class_l, 0.0), axis=1, keepdims=True)
    rank_s = jnp.sum(jnp.where((class_s == class_l) & (qb < qa), 1.0, 0.0), axis=1, keepdims=True)
    rank_i = rank_s.astype(I32)
    found = class_s.astype(I32) * 16 + (rank_i & 15)
    for h in range(2):
        s5[h] = jnp.where((qb == found) & ((rank_i >> 4) == h), 1.0, 0.0).astype(BF16)

    load_right.wait()
    right_f[...] = right_v[...].reshape(512, 64)
    base = 2 * lax.rem(r, 4)
    right_t = jnp.concatenate(
        [right_f[pl.ds(base + h, 64, stride=8), :] for h in range(2)], axis=0).T

    ring_hop(3)
    load_ranks.wait()

    k_of = iota((64, 128), 0)
    for jj in range(4):
        way = jj % 2
        hop(jj, slot_of(way, 4), right, way, 3).wait_recv()
        loads[2 * jj].wait()
        loads[2 * jj + 1].wait()
        g = gath[jj].reshape(512, 128)
        pair = [dot(basis_v[2 * jj + h], g) for h in range(2)]
        for i in range(16):
            at = slice(i * 64, (i + 1) * 64)
            limit = jnp.where(low, ranks_s[2 * jj, i], ranks_s[2 * jj + 1, i])
            both = jnp.where(low, pair[0][at], pair[1][at])
            cm[i, jj * 64:(jj + 1) * 64, :] = jnp.where(k_of < limit, both, 0.0).astype(BF16)

    def update(to):
        sums = []
        for h in range(2):
            u = dot_tn(w0[2 * to + h], cm[2 * to + h])
            sums.append(jnp.where(low, u[0:64], u[64:128]))
        return jnp.where(low, sums[0], sums[1]) + swap(jnp.where(low, sums[1], sums[0]))

    def p2(d, to):
        return remote(msg.at[d], part.at[d], p2_send.at[d], p2_recv.at[d], "row", to)

    for d in range(1, N):
        to = lax.rem(r + d, N)
        msg[d] = update(to).astype(BF16)
        p2(d, to).start()
    acc = right_t - update(r)

    load_inv.wait()
    for d in range(1, N):
        remote(inv_ref.at[pl.ds(2 * r, 2)], invg.at[r], inv_send.at[d], inv_recv.at[d], "row", r).wait_recv()
    for h in range(2):
        invl[h * 64:(h + 1) * 64, :] = invg[:, h].astype(F32).reshape(64, 512).astype(BF16)

    for d in range(1, N):
        p2(d, r).wait_recv()
        acc = acc - part[d].astype(F32)
    red[...] = acc.astype(BF16)
    redg[c] = acc.astype(BF16)

    def p3(d, to):
        return remote(red, redg.at[c], p3_send.at[d], p3_recv.at[d], "col", to)

    for d in range(1, N):
        p3(d, lax.rem(c + d, N)).start()
    for d in range(1, N):
        p3(d, c).wait_recv()

    s = dot(invl[...], redg[...].reshape(512, 128))
    solved = jnp.where(low, s[0:64], s[64:128]).astype(BF16)
    solg[r] = solved

    def p4(d, to):
        return remote(solg.at[r], solg.at[r], p4_send.at[d], p4_recv.at[d], "row", to)

    for d in range(1, N):
        p4(d, lax.rem(r + d, N)).start()
    for d in range(1, N):
        p4(d, r).wait_recv()

    picked = dot(selm[...], solg[...].reshape(512, 128))
    rows = jnp.where(low, picked[0:256], picked[256:512])
    rows = (rows + swap(rows)).reshape(8, 32, 128)
    pk[...] = jnp.where(low, rows[:, 0:16], rows[:, 16:32]).astype(BF16)
    chg[c] = pk[c]

    def p5(d, to):
        return remote(pk.at[to], chg.at[c], p5_send.at[d], p5_recv.at[d], "col", to)

    for d in range(1, N):
        p5(d, lax.rem(c + d, N)).start()

    own_rows = picked[512:576]
    out_sol[:, 0] = own_rows[:, 0:64].reshape(8, 8, 64).astype(BF16)
    out_sol[:, 1] = swap(own_rows)[:, 0:64].reshape(8, 8, 64).astype(BF16)

    for d in range(1, N):
        p5(d, c).wait_recv()
    got = chg[...].reshape(128, 128)
    child = jnp.where(low, dot(s5[0], got), dot(s5[1], got))
    child = child + swap(child)
    out_child[...] = child.T[0:64].astype(BF16)

    for jj in range(4):
        for step in range(4):
            for way in range(2):
                if step < 3 or jj % 2 == way:
                    hop(jj, c, right, way, step).wait_send()
    for d in range(1, N):
        remote(inv_ref.at[pl.ds(2 * r, 2)], invg.at[r], inv_send.at[d], inv_recv.at[d], "row", r).wait_send()
        p2(d, r).wait_send()
        p3(d, c).wait_send()
        p4(d, r).wait_send()
        p5(d, c).wait_send()


def on_device(right_side, rest_solution, rest_basis, window_basis, ranks, inverses, child_map):
    any_spec = pl.BlockSpec(memory_space=pl.ANY)
    vmem_spec = pl.BlockSpec(memory_space=pltpu.VMEM)
    dma = pltpu.SemaphoreType.DMA
    sol, child = pl.pallas_call(
        kernel,
        out_shape=(
            jax.ShapeDtypeStruct((8, 2, 8, 64), BF16),
            jax.ShapeDtypeStruct((64, 128), BF16),
        ),
        in_specs=[any_spec] * 7,
        out_specs=(vmem_spec, vmem_spec),
        scratch_shapes=[
            pltpu.VMEM((64, 8, 64), BF16),
            pltpu.VMEM((512, 64), F32),
            pltpu.VMEM((64, 8, 64), F32),
            pltpu.VMEM((512, 64), F32),
            pltpu.VMEM((8, 1024, 512), BF16),
            pltpu.VMEM((8, 64, 16, 64), BF16),
            pltpu.VMEM((2, 512), I32),
            pltpu.SMEM((8, 16), I32),
            pltpu.VMEM((4, 8, 64, 128), BF16),
            pltpu.VMEM((16, 256, 128), BF16),
            pltpu.VMEM((16, 256, 128), BF16),
            pltpu.VMEM((8, 64, 128), BF16),
            pltpu.VMEM((8, 64, 128), BF16),
            pltpu.VMEM((64, 128), BF16),
            pltpu.VMEM((8, 64, 128), BF16),
            pltpu.VMEM((8, 2, 8, 512), BF16),
            pltpu.VMEM((128, 512), BF16),
            pltpu.VMEM((8, 64, 128), BF16),
            pltpu.VMEM((576, 512), BF16),
            pltpu.VMEM((2, 128, 128), BF16),
            pltpu.VMEM((8, 16, 128), BF16),
            pltpu.VMEM((8, 16, 128), BF16),
            dma((6,)), dma((8,)), dma((2, 4, 4)), dma((2, 4, 4)),
            dma((8,)), dma((8,)),
            dma((8,)), dma((8,)), dma((8,)), dma((8,)),
            dma((8,)), dma((8,)), dma((8,)), dma((8,)),
        ],
        compiler_params=pltpu.CompilerParams(
            collective_id=0, has_side_effects=True, vmem_limit_bytes=56 * 1024 * 1024
        ),
        cost_estimate=pl.CostEstimate(flops=700_000_000, bytes_accessed=12_000_000, transcendentals=0),
    )(right_side, rest_solution, rest_basis, window_basis, ranks, inverses, child_map)
    solution_rows = sol.reshape(16, 8, 64).transpose(2, 0, 1)
    return solution_rows, child.reshape(64, 2, 64)


def solution(mesh):
    in_specs = (
        P("shot", None, "col"),
        P("shot", "row", "col"),
        P("row", None, None),
        P("row", None, None, "col"),
        P("row", None),
        P(None, ("row", "col"), None),
        P(),
    )
    out_specs = (P("shot", None, ("row", "col")), P("shot", None, ("row", "col")))
    return jax.shard_map(
        on_device, mesh=mesh, in_specs=in_specs, out_specs=out_specs, check_vma=False
    )
```

time: 245 us -> 49.9 us (0.20)
  waiting for transfers between devices: 181 us -> 0 us
  Pallas kernels: 0 us -> 46.3 us
  blocking collectives: 25.7 us -> 0 us
  between operations: 13.8 us -> 0.64 us
  matrix products: 10.6 us -> 0 us
  local copies, waits for them, and re-layouts: 8.25 us -> 2.79 us
  other arithmetic: 4.61 us -> 0 us
    all_gather x2 -> x0, waiting for transfers between devices: 114 us -> none  [the longest x1 74.8 us: on_device(): gathered_rows = lax.all_gather(solution, ('row', 'col'), axis=2, tiled=True)]
    psum x1 -> x0, waiting for transfers between devices: 67.6 us -> none  [on_device(): lax.psum(partial_update.astype(jnp.bfloat16), 'row').astype(jnp.float32)]
    pallas_call x0 -> x1, Pallas kernels: none -> 46.3 us  [on_device(): pl.pallas_call(kernel, out_shape=(jax.ShapeDtypeStruct((8, 2, 8, 64), BF1...]
    all_gather x1 -> x0, blocking collectives: 25.7 us -> none  [on_device(): lax.all_gather(rest_solution, 'col', axis=2, tiled=True)]
    dot_general x3 -> x0, matrix products: 10.6 us -> none  [the longest x1 6.04 us: on_device(): jnp.einsum('jap,sjp->jas', rest_basis, lax.all_gather(rest_solution, 'col...]
    convert_element_type x2 -> x0, other arithmetic: 3.76 us -> none  [the longest x1 2.06 us: on_device(): jnp.where(rank_mask[..., None], coeffs, jnp.float32(0.0))]
    gather x2 -> x0, local copies, waits for them, and re-layouts: 3.23 us -> none  [on_device(): child_values = flat_rows[:, own_map]]
  transfers between devices with their start and end apart: 3 -> 0, of which waited for: 3 -> 0; matrix products, arithmetic and copies ran while one was open for 0% -> 0% of each run, Pallas kernels for 0% -> 0%
where the time goes in v1:
time: 49.9 us; the launch traced here: 49.7 us
  Pallas kernels  46.3 us (93%)
  local copies, waits for them, and re-layouts  2.79 us (6%)
  between operations  0.64 us (1%)
    pallas_call x1, Pallas kernels, on_device(): pl.pallas_call(kernel, out_shape=(jax.ShapeDtypeStruct((8, 2, 8, 64), BF1...  46.3 us
    reshape x1, local copies, waits for them, and re-layouts, on_device(): return (solution_rows, child.reshape(64, 2, 64))  1.41 us
    unnamed x1, local copies, waits for them, and re-layouts  1.37 us

profile of v1, /device:TPU:1, one launch (start us, length us, event | category | flops | bytes accessed | tf_op | source)
XLA Modules:
  0.0 49.7 jit_solution(10146404420646029623)
XLA Ops:
  0.6 46.3 %shard_map.86 = (bf16[8,2,8,64]{3,2,1,0:T(8,128)(2,1)}, bf16[64,128]{1,0:T(8,128)(2,1)}) custom-call(f32[64,16,64]{2,1,0:T(8,128)} %right_ref.1, bf16[64,8,64]{2,1,0:T(8,128)(2,1)} %sol_ref.1, bf16[8,1024,512]{2,1,0:T(8,128)(2,1)} %basis_ref.1, bf16[8,64,16,64]{3,2,1,0:T(8,128)(2,1)} %wb_ref.1, s32[8,16]{1,0:T(8,128)} %ranks_ref.1, ...), custom_call_target="tpu_custom_call" | custom-call | flops 700000000 | bytes 12000000 | tf_op jit(solution)/shard_map/pallas_call | solution.py:283
  46.9 1.4 %reshape.11 = bf16[64,2,64]{2,1,0:T(2,128)(2,1)} reshape(bf16[64,128]{1,0:T(8,128)(2,1)} %get-tuple-element.5) | data formatting | bytes 32768 | tf_op jit(solution)/shard_map/reshape | solution.py:325
  48.3 1.4 %copy.10 = bf16[64,16,8]{0,2,1:T(8,128)(2,1)} copy(bf16[64,16,8]{0,2,1:T(8,128)(2,1)} %bitcast.3) | data formatting | bytes 32768

commit v2 on v1

--- a/solution.py
+++ b/solution.py
@@ -10,6 +10,8 @@
 BF16 = jnp.bfloat16
 I32 = jnp.int32
 N = 8
+NEAR = (2, 6, 1, 7)
+FAR_FIRST = (4, 3, 5, 2, 6, 1, 7)
 
 
 def iota(shape, axis):
@@ -18,10 +20,6 @@
 
 def dot(a, b):
     return jnp.dot(a, b, preferred_element_type=F32)
-
-
-def dot_tn(a, b):
-    return lax.dot_general(a, b, (((0,), (0,)), ((), ())), preferred_element_type=F32)
 
 
 def swap(x):
@@ -32,34 +30,37 @@
     right_ref, sol_ref, basis_ref, wb_ref, ranks_ref, inv_ref, map_ref,
     out_sol, out_child,
     sol_v, sol_f, right_v, right_f, basis_v, wb_v, map_v, ranks_s,
-    gath, w0, cm, msg, part, red, redg, invg, invl, solg, selm, s5, pk, chg,
+    gath, w0, wt, cm, msg, part, red, redg, invg, invl, solg, selm, s5, pk, chg,
     load_sem, basis_sem, ring_send, ring_recv, inv_send, inv_recv,
     p2_send, p2_recv, p3_send, p3_recv, p4_send, p4_recv, p5_send, p5_recv,
 ):
     r = lax.axis_index("row")
     c = lax.axis_index("col")
-    right, left = lax.rem(c + 1, N), lax.rem(c + N - 1, N)
-
-    def remote(src, dst, send, recv, axis, to):
+
+    def remote(src, dst, send, recv, at, axis, to):
         return pltpu.make_async_remote_copy(
-            src_ref=src, dst_ref=dst, send_sem=send, recv_sem=recv,
+            src_ref=src, dst_ref=dst, send_sem=send.at[at], recv_sem=recv.at[at],
             device_id={axis: to}, device_id_type=MESH,
         )
 
-    load_sol = pltpu.make_async_copy(sol_ref, sol_v, load_sem.at[0])
+    def local(src, dst, sem, at):
+        return pltpu.make_async_copy(src, dst, sem.at[at])
+
+    load_sol = local(sol_ref, sol_v, load_sem, 0)
     load_sol.start()
-    load_wb = pltpu.make_async_copy(wb_ref, wb_v, load_sem.at[1])
-    load_map = pltpu.make_async_copy(
-        map_ref.at[:, pl.ds(pl.multiple_of(r * 512, 512), 512)], map_v, load_sem.at[2])
-    load_ranks = pltpu.make_async_copy(ranks_ref, ranks_s, load_sem.at[3])
-    load_right = pltpu.make_async_copy(
-        right_ref.at[:, pl.ds(pl.multiple_of((r // 4) * 8, 8), 8), :], right_v, load_sem.at[4])
-    load_inv = pltpu.make_async_copy(
-        inv_ref.at[pl.ds(2 * r, 2)], invg.at[r], load_sem.at[5])
+    load_wb = local(wb_ref, wb_v, load_sem, 1)
+    load_map = local(
+        map_ref.at[:, pl.ds(pl.multiple_of(r * 512, 512), 512)], map_v, load_sem, 2)
+    load_ranks = local(ranks_ref, ranks_s, load_sem, 3)
+    load_right = local(
+        right_ref.at[:, pl.ds(pl.multiple_of((r // 4) * 8, 8), 8), :], right_v, load_sem, 4)
+    load_inv = local(
+        inv_ref.at[pl.ds(2 * r, 2)], invg.at[r], load_sem, 5)
 
     barrier = pltpu.get_barrier_semaphore()
-    for d in range(1, N):
+    for d in NEAR:
         pl.semaphore_signal(barrier, inc=1, device_id={"col": lax.rem(c + d, N)}, device_id_type=MESH)
+    for d in FAR_FIRST:
         pl.semaphore_signal(barrier, inc=1, device_id={"row": lax.rem(r + d, N)}, device_id_type=MESH)
 
     load_wb.start()
@@ -68,7 +69,7 @@
     load_right.start()
     load_inv.start()
     loads = [
-        pltpu.make_async_copy(basis_ref.at[j], basis_v.at[j], basis_sem.at[j])
+        local(basis_ref.at[j], basis_v.at[j], basis_sem, j)
         for j in range(N)
     ]
     for load in loads:
@@ -81,27 +82,32 @@
             [sol_f[pl.ds(2 * jj + h, 64, stride=8), :] for h in range(2)], axis=0)
         gath[jj, c] = both.T.astype(BF16)
 
-    pl.semaphore_wait(barrier, 2 * (N - 1))
-
-    def hop(jj, slot, to, way, step):
-        return remote(gath.at[jj, slot], gath.at[jj, slot],
-                      ring_send.at[way, step, jj], ring_recv.at[way, step, jj], "col", to)
-
-    def slot_of(way, step):
-        return lax.rem(c + (N - step if way == 0 else step), N)
-
-    def ring_hop(step):
-        for jj in range(4):
-            for way in range(2):
-                if step > 0:
-                    hop(jj, slot_of(way, step), right, way, step - 1).wait_recv()
-                if step < 3 or jj % 2 == way:
-                    hop(jj, slot_of(way, step), (right, left)[way], way, step).start()
-
-    ring_hop(0)
-    for d in range(1, N):
+    pl.semaphore_wait(barrier, len(NEAR) + len(FAR_FIRST))
+
+    def chunk(jj, slot, to, lane):
+        slot, to = lax.rem(c + slot + N, N), lax.rem(c + to + N, N)
+        return remote(gath.at[jj, slot], gath.at[jj, slot], ring_send, ring_recv, (lane, jj), "col", to)
+
+    for jj in range(4):
+        chunk(jj, 0, 2, 0).start()
+        chunk(jj, 0, -2, 1).start()
+    for jj in range(4):
+        chunk(jj, 0, 1, 2).start()
+        chunk(jj, 0, -1, 3).start()
+
+    def relay(jj):
+        chunk(jj, -2, 2, 0).wait_recv()
+        if jj % 2 == 0:
+            chunk(jj, -2, 2, 6).start()
+        chunk(jj, -2, 1, 4).start()
+        chunk(jj, 2, -2, 1).wait_recv()
+        if jj % 2 == 1:
+            chunk(jj, 2, -2, 6).start()
+        chunk(jj, 2, -1, 5).start()
+
+    for d in FAR_FIRST:
         to = lax.rem(r + d, N)
-        remote(inv_ref.at[pl.ds(2 * to, 2)], invg.at[r], inv_send.at[d], inv_recv.at[d], "row", to).start()
+        remote(inv_ref.at[pl.ds(2 * to, 2)], invg.at[r], inv_send, inv_recv, d, "row", to).start()
 
     load_wb.wait()
     row_i, col_i = iota((256, 256), 0), iota((256, 256), 1)
@@ -116,12 +122,12 @@
         y = dot(perm, x).astype(BF16).reshape(16, 16, 128)
         w0[:, pl.ds(pl.multiple_of(jj * 64 + kb * 16, 16), 16), :] = y
 
-    for step in range(8):
+    for step in range(16):
         regroup(step)
-    ring_hop(1)
-    for step in range(8, 16):
-        regroup(step)
-    ring_hop(2)
+    for jj in range(4):
+        relay(jj)
+    for i in range(16):
+        wt[i] = w0[i].T
 
     low = iota((1, 128), 1) < 64
     load_map.wait()
@@ -175,13 +181,12 @@
     right_t = jnp.concatenate(
         [right_f[pl.ds(base + h, 64, stride=8), :] for h in range(2)], axis=0).T
 
-    ring_hop(3)
     load_ranks.wait()
 
     k_of = iota((64, 128), 0)
     for jj in range(4):
-        way = jj % 2
-        hop(jj, slot_of(way, 4), right, way, 3).wait_recv()
+        for lane in (2, 3, 4, 5, 6):
+            chunk(jj, 0, 1, lane).wait_recv()
         loads[2 * jj].wait()
         loads[2 * jj + 1].wait()
         g = gath[jj].reshape(512, 128)
@@ -195,22 +200,23 @@
     def update(to):
         sums = []
         for h in range(2):
-            u = dot_tn(w0[2 * to + h], cm[2 * to + h])
+            u = dot(wt[2 * to + h], cm[2 * to + h])
             sums.append(jnp.where(low, u[0:64], u[64:128]))
         return jnp.where(low, sums[0], sums[1]) + swap(jnp.where(low, sums[1], sums[0]))
 
     def p2(d, to):
-        return remote(msg.at[d], part.at[d], p2_send.at[d], p2_recv.at[d], "row", to)
-
-    for d in range(1, N):
-        to = lax.rem(r + d, N)
-        msg[d] = update(to).astype(BF16)
-        p2(d, to).start()
+        return remote(msg.at[d], part.at[d], p2_send, p2_recv, d, "row", to)
+
+    for batch in (FAR_FIRST[:4], FAR_FIRST[4:]):
+        for d in batch:
+            msg[d] = update(lax.rem(r + d, N)).astype(BF16)
+        for d in batch:
+            p2(d, lax.rem(r + d, N)).start()
     acc = right_t - update(r)
 
     load_inv.wait()
     for d in range(1, N):
-        remote(inv_ref.at[pl.ds(2 * r, 2)], invg.at[r], inv_send.at[d], inv_recv.at[d], "row", r).wait_recv()
+        remote(inv_ref.at[pl.ds(2 * r, 2)], invg.at[r], inv_send, inv_recv, d, "row", r).wait_recv()
     for h in range(2):
         invl[h * 64:(h + 1) * 64, :] = invg[:, h].astype(F32).reshape(64, 512).astype(BF16)
 
@@ -221,9 +227,9 @@
     redg[c] = acc.astype(BF16)
 
     def p3(d, to):
-        return remote(red, redg.at[c], p3_send.at[d], p3_recv.at[d], "col", to)
-
-    for d in range(1, N):
+        return remote(red, redg.at[c], p3_send, p3_recv, d, "col", to)
+
+    for d in FAR_FIRST:
         p3(d, lax.rem(c + d, N)).start()
     for d in range(1, N):
         p3(d, c).wait_recv()
@@ -233,9 +239,9 @@
     solg[r] = solved
 
     def p4(d, to):
-        return remote(solg.at[r], solg.at[r], p4_send.at[d], p4_recv.at[d], "row", to)
-
-    for d in range(1, N):
+        return remote(solg.at[r], solg.at[r], p4_send, p4_recv, d, "row", to)
+
+    for d in FAR_FIRST:
         p4(d, lax.rem(r + d, N)).start()
     for d in range(1, N):
         p4(d, r).wait_recv()
@@ -247,9 +253,9 @@
     chg[c] = pk[c]
 
     def p5(d, to):
-        return remote(pk.at[to], chg.at[c], p5_send.at[d], p5_recv.at[d], "col", to)
-
-    for d in range(1, N):
+        return remote(pk.at[to], chg.at[c], p5_send, p5_recv, d, "col", to)
+
+    for d in FAR_FIRST:
         p5(d, lax.rem(c + d, N)).start()
 
     own_rows = picked[512:576]
@@ -264,12 +270,10 @@
     out_child[...] = child.T[0:64].astype(BF16)
 
     for jj in range(4):
-        for step in range(4):
-            for way in range(2):
-                if step < 3 or jj % 2 == way:
-                    hop(jj, c, right, way, step).wait_send()
-    for d in range(1, N):
-        remote(inv_ref.at[pl.ds(2 * r, 2)], invg.at[r], inv_send.at[d], inv_recv.at[d], "row", r).wait_send()
+        for lane in range(7):
+            chunk(jj, 0, 1, lane).wait_send()
+    for d in range(1, N):
+        remote(inv_ref.at[pl.ds(2 * r, 2)], invg.at[r], inv_send, inv_recv, d, "row", r).wait_send()
         p2(d, r).wait_send()
         p3(d, c).wait_send()
         p4(d, r).wait_send()
@@ -283,8 +287,8 @@
     sol, child = pl.pallas_call(
         kernel,
         out_shape=(
-            jax.ShapeDtypeStruct((8, 2, 8, 64), BF16),
-            jax.ShapeDtypeStruct((64, 128), BF16),
+            pltpu.VMEM((8, 2, 8, 64), BF16),
+            pltpu.VMEM((64, 128), BF16),
         ),
         in_specs=[any_spec] * 7,
         out_specs=(vmem_spec, vmem_spec),
@@ -299,6 +303,7 @@
             pltpu.SMEM((8, 16), I32),
             pltpu.VMEM((4, 8, 64, 128), BF16),
             pltpu.VMEM((16, 256, 128), BF16),
+            pltpu.VMEM((16, 128, 256), BF16),
             pltpu.VMEM((16, 256, 128), BF16),
             pltpu.VMEM((8, 64, 128), BF16),
             pltpu.VMEM((8, 64, 128), BF16),
@@ -311,7 +316,7 @@
             pltpu.VMEM((2, 128, 128), BF16),
             pltpu.VMEM((8, 16, 128), BF16),
             pltpu.VMEM((8, 16, 128), BF16),
-            dma((6,)), dma((8,)), dma((2, 4, 4)), dma((2, 4, 4)),
+            dma((6,)), dma((8,)), dma((7, 4)), dma((7, 4)),
             dma((8,)), dma((8,)),
             dma((8,)), dma((8,)), dma((8,)), dma((8,)),
             dma((8,)), dma((8,)), dma((8,)), dma((8,)),

time: 49.9 us -> 41.3 us (0.83)
  Pallas kernels: 46.3 us -> 39.1 us
  local copies, waits for them, and re-layouts: 2.79 us -> 1.31 us
    pallas_call x1, Pallas kernels: 46.3 us -> 39.1 us  [on_device(): pl.pallas_call(kernel, out_shape=(pltpu.VMEM((8, 2, 8, 64), BF16), pltpu....]
    unnamed x1, local copies, waits for them, and re-layouts: 1.37 us -> 0.62 us
    reshape x1, local copies, waits for them, and re-layouts: 1.41 us -> 0.7 us  [on_device(): return (solution_rows, child.reshape(64, 2, 64))]
where the time goes in v2:
time: 41.3 us; the launch traced here: 41 us
  Pallas kernels  39.1 us (95%)
  local copies, waits for them, and re-layouts  1.31 us (3%)
  between operations  0.64 us (2%)
    pallas_call x1, Pallas kernels, on_device(): pl.pallas_call(kernel, out_shape=(pltpu.VMEM((8, 2, 8, 64), BF16), pltpu....  39.1 us

profile of v2, /device:TPU:1, one launch (start us, length us, event | category | flops | bytes accessed | tf_op | source)
XLA Modules:
  0.0 41.0 jit_solution(11619603016253825309)
XLA Ops:
  0.6 39.1 %shard_map.86 = (bf16[8,2,8,64]{3,2,1,0:T(8,128)(2,1)S(1)}, bf16[64,128]{1,0:T(8,128)(2,1)S(1)}) custom-call(f32[64,16,64]{2,1,0:T(8,128)} %right_ref.1, bf16[64,8,64]{2,1,0:T(8,128)(2,1)} %sol_ref.1, bf16[8,1024,512]{2,1,0:T(8,128)(2,1)} %basis_ref.1, bf16[8,64,16,64]{3,2,1,0:T(8,128)(2,1)} %wb_ref.1, s32[8,16]{1,0:T(8,128)} %ranks_ref.1, ...), custom_call_target="tpu_custom_call" | custom-call | flops 700000000 | bytes 12000000 | tf_op jit(solution)/shard_map/pallas_call | solution.py:287
  39.7 0.6 %copy.10 = bf16[64,16,8]{0,2,1:T(8,128)(2,1)} copy(bf16[64,16,8]{0,2,1:T(8,128)(2,1)S(1)} %bitcast.3) | data formatting | bytes 32768
  40.3 0.7 %reshape.11 = bf16[64,2,64]{2,1,0:T(2,128)(2,1)} reshape(bf16[64,128]{1,0:T(8,128)(2,1)S(1)} %get-tuple-element.5) | data formatting | bytes 32768 | tf_op jit(solution)/shard_map/reshape | solution.py:330

commit v3 on v2

--- a/solution.py
+++ b/solution.py
@@ -30,9 +30,9 @@
     right_ref, sol_ref, basis_ref, wb_ref, ranks_ref, inv_ref, map_ref,
     out_sol, out_child,
     sol_v, sol_f, right_v, right_f, basis_v, wb_v, map_v, ranks_s,
-    gath, w0, wt, cm, msg, part, red, redg, invg, invl, solg, selm, s5, pk, chg,
+    gath, w0, wt, cm, msg, part, red, redg, invg, invz, solv, selm, out_msg, fin,
     load_sem, basis_sem, ring_send, ring_recv, inv_send, inv_recv,
-    p2_send, p2_recv, p3_send, p3_recv, p4_send, p4_recv, p5_send, p5_recv,
+    p2_send, p2_recv, p3_send, p3_recv, p4_send, p4_recv, tile_send, tile_recv,
 ):
     r = lax.axis_index("row")
     c = lax.axis_index("col")
@@ -49,8 +49,7 @@
     load_sol = local(sol_ref, sol_v, load_sem, 0)
     load_sol.start()
     load_wb = local(wb_ref, wb_v, load_sem, 1)
-    load_map = local(
-        map_ref.at[:, pl.ds(pl.multiple_of(r * 512, 512), 512)], map_v, load_sem, 2)
+    load_map = local(map_ref, map_v, load_sem, 2)
     load_ranks = local(ranks_ref, ranks_s, load_sem, 3)
     load_right = local(
         right_ref.at[:, pl.ds(pl.multiple_of((r // 4) * 8, 8), 8), :], right_v, load_sem, 4)
@@ -129,51 +128,49 @@
     for i in range(16):
         wt[i] = w0[i].T
 
+    load_inv.wait()
+    for d in range(1, N):
+        remote(inv_ref.at[pl.ds(2 * r, 2)], invg.at[r], inv_send, inv_recv, d, "row", r).wait_recv()
+    for h in range(2):
+        invz[c, h] = invg[:, h].astype(F32).reshape(64, 512).astype(BF16)
+
+    def tile_part(h, slot, to, lane):
+        slot, to = lax.rem(c + slot + N, N), lax.rem(c + to + N, N)
+        return remote(invz.at[slot, h], invz.at[slot, h], tile_send, tile_recv, (lane, h), "col", to)
+
+    for h in range(2):
+        tile_part(h, 0, 2, 0).start()
+        tile_part(h, 0, -2, 1).start()
+    for h in range(2):
+        tile_part(h, 0, 1, 2).start()
+        tile_part(h, 0, -1, 3).start()
+
+    def tile_relay(h):
+        tile_part(h, -2, 2, 0).wait_recv()
+        tile_part(h, 2, -2, 1).wait_recv()
+        if h == 0:
+            tile_part(h, -2, 2, 6).start()
+        else:
+            tile_part(h, 2, -2, 6).start()
+        tile_part(h, -2, 1, 4).start()
+        tile_part(h, 2, -1, 5).start()
+
     low = iota((1, 128), 1) < 64
     load_map.wait()
-    w = map_v[...]
-    cc = (w >> 3) & 7
-    code = (((w >> 9) & 1) << 9) + ((w >> 10) << 6) + (((w >> 6) & 7) << 3) + (w & 7) + 1
-    mine = cc == c
-    mine_f = jnp.where(mine, 1.0, 0.0)
-    mine8 = jnp.where(iota((8, 512), 0) == 0, mine_f[0:1], mine_f[1:2]).astype(BF16)
-    ta, tb = iota((512, 512), 0), iota((512, 512), 1)
-    same = (ta >> 6) == (tb >> 6)
-    before = dot(mine8, jnp.where(same & (ta < tb), 1.0, 0.0).astype(BF16))
-    total = dot(mine8, jnp.where(same, 1.0, 0.0).astype(BF16))
-    place = (before[0:1].astype(I32), (before[1:2] + total[0:1]).astype(I32))
-    code_f = jnp.where(mine, code, 0).astype(F32)
-    slots = []
-    for g in range(4):
-        at = slice(g * 128, (g + 1) * 128)
-        ra, la = iota((64, 128), 0), iota((64, 128), 1)
-        ours = (ra >> 5) == (la >> 6)
-        acc = jnp.zeros((64, 128), F32)
-        for ch in range(2):
-            take = ours & ((ra & 31) == place[ch][:, at])
-            acc = acc + jnp.where(take, code_f[ch:ch + 1, at], 0.0)
-        slots.append(jnp.sum(acc, axis=1, keepdims=True))
-    slot = jnp.concatenate(slots, axis=0).astype(I32)
-    src = iota((256, 512), 1) + 1
-    for h in range(2):
-        selm[h * 256:(h + 1) * 256, :] = jnp.where(src + h * 512 == slot, 1.0, 0.0).astype(BF16)
-    ra, la = iota((64, 512), 0), iota((64, 512), 1)
-    selm[512:576, :] = jnp.where(
-        la == ((ra >> 3) << 6) + r * 8 + (ra & 7), 1.0, 0.0).astype(BF16)
-
-    x = map_v[:, pl.ds(pl.multiple_of((c // 2) * 128, 128), 128)]
-    x_swapped = swap(x)
     odd = lax.rem(c, 2) == 1
-    own = jnp.where(
-        low, jnp.where(odd, x_swapped[0:1], x[0:1]), jnp.where(odd, x[1:2], x_swapped[1:2]))
-    class_l = ((own >> 3) & 7).astype(F32)
-    qa, qb = iota((128, 128), 0), iota((128, 128), 1)
-    class_s = jnp.sum(jnp.where(qa == qb, class_l, 0.0), axis=1, keepdims=True)
-    rank_s = jnp.sum(jnp.where((class_s == class_l) & (qb < qa), 1.0, 0.0), axis=1, keepdims=True)
-    rank_i = rank_s.astype(I32)
-    found = class_s.astype(I32) * 16 + (rank_i & 15)
-    for h in range(2):
-        s5[h] = jnp.where((qb == found) & ((rank_i >> 4) == h), 1.0, 0.0).astype(BF16)
+    own = []
+    for to in range(N):
+        x = map_v[:, pl.ds(pl.multiple_of((to * 4 + c // 2) * 128, 128), 128)]
+        own.append(jnp.where(odd, swap(x), x))
+    w = jnp.concatenate(own, axis=0)
+    place = (((w >> 3) & 7) << 6) + (((w >> 6) & 7) << 3) + (w & 7)
+    code = jnp.where((w >> 10) == r, place + (((w >> 9) & 1) << 9), -1)
+    codes = jnp.concatenate([code.astype(F32), jnp.zeros((112, 128), F32)], axis=0).T.astype(I32)
+    src = iota((64, 512), 1)
+    for k in range(16):
+        slot = codes[0:64, k:k + 1]
+        for h in range(2):
+            selm[h, k * 64:(k + 1) * 64, :] = jnp.where(src + h * 512 == slot, 1.0, 0.0).astype(BF16)
 
     load_right.wait()
     right_f[...] = right_v[...].reshape(512, 64)
@@ -214,11 +211,8 @@
             p2(d, lax.rem(r + d, N)).start()
     acc = right_t - update(r)
 
-    load_inv.wait()
-    for d in range(1, N):
-        remote(inv_ref.at[pl.ds(2 * r, 2)], invg.at[r], inv_send, inv_recv, d, "row", r).wait_recv()
-    for h in range(2):
-        invl[h * 64:(h + 1) * 64, :] = invg[:, h].astype(F32).reshape(64, 512).astype(BF16)
+    for h in range(2):
+        tile_relay(h)
 
     for d in range(1, N):
         p2(d, r).wait_recv()
@@ -234,40 +228,44 @@
     for d in range(1, N):
         p3(d, c).wait_recv()
 
-    s = dot(invl[...], redg[...].reshape(512, 128))
-    solved = jnp.where(low, s[0:64], s[64:128]).astype(BF16)
-    solg[r] = solved
+    for h in range(2):
+        for lane in (2, 3, 4, 5, 6):
+            tile_part(h, 0, 1, lane).wait_recv()
+    g = redg[...].reshape(512, 128)
+    s = [dot(invz[:, h].reshape(512, 512), g) for h in range(2)]
+    solved = jnp.where(low, s[0], s[1])
+    solv[...] = solved
+    solved = solved.astype(BF16)
 
     def p4(d, to):
-        return remote(solg.at[r], solg.at[r], p4_send, p4_recv, d, "row", to)
-
-    for d in FAR_FIRST:
-        p4(d, lax.rem(r + d, N)).start()
+        return remote(out_msg.at[to], fin.at[r], p4_send, p4_recv, d, "row", to)
+
+    def pick(to):
+        at = pl.ds(pl.multiple_of(to * 128, 128), 128)
+        rows = jnp.where(low, dot(selm[0, at, :], solved), dot(selm[1, at, :], solved))
+        rows = rows + swap(rows)
+        out_msg[to, 0:64, :] = jnp.where(low, rows[0:64], rows[64:128]).astype(BF16)
+        mine = solv[pl.ds(pl.multiple_of(c * 64 + to * 8, 8), 8), :]
+        out_msg[to, 64:80, :] = jnp.concatenate([mine, mine], axis=0).astype(BF16)
+
+    for batch in (FAR_FIRST[:4], FAR_FIRST[4:]):
+        for d in batch:
+            pick(lax.rem(r + d, N))
+        for d in batch:
+            p4(d, lax.rem(r + d, N)).start()
+    pick(r)
+    fin[r] = out_msg[r]
     for d in range(1, N):
         p4(d, r).wait_recv()
 
-    picked = dot(selm[...], solg[...].reshape(512, 128))
-    rows = jnp.where(low, picked[0:256], picked[256:512])
-    rows = (rows + swap(rows)).reshape(8, 32, 128)
-    pk[...] = jnp.where(low, rows[:, 0:16], rows[:, 16:32]).astype(BF16)
-    chg[c] = pk[c]
-
-    def p5(d, to):
-        return remote(pk.at[to], chg.at[c], p5_send, p5_recv, d, "col", to)
-
-    for d in FAR_FIRST:
-        p5(d, lax.rem(c + d, N)).start()
-
-    own_rows = picked[512:576]
-    out_sol[:, 0] = own_rows[:, 0:64].reshape(8, 8, 64).astype(BF16)
-    out_sol[:, 1] = swap(own_rows)[:, 0:64].reshape(8, 8, 64).astype(BF16)
-
-    for d in range(1, N):
-        p5(d, c).wait_recv()
-    got = chg[...].reshape(128, 128)
-    child = jnp.where(low, dot(s5[0], got), dot(s5[1], got))
-    child = child + swap(child)
-    out_child[...] = child.T[0:64].astype(BF16)
+    child = jnp.zeros((64, 128), F32)
+    for k in range(N):
+        child = child + fin[k, 0:64, :].astype(F32)
+        rows = fin[k, 64:80, :].astype(F32)
+        out_sol[k, 0] = rows[0:8, 0:64].astype(BF16)
+        out_sol[k, 1] = swap(rows)[0:8, 0:64].astype(BF16)
+    child = child.T
+    out_child[...] = jnp.concatenate([child[0:64], child[64:128]], axis=1).astype(BF16)
 
     for jj in range(4):
         for lane in range(7):
@@ -277,7 +275,9 @@
         p2(d, r).wait_send()
         p3(d, c).wait_send()
         p4(d, r).wait_send()
-        p5(d, c).wait_send()
+    for h in range(2):
+        for lane in range(7):
+            tile_part(h, 0, 1, lane).wait_send()
 
 
 def on_device(right_side, rest_solution, rest_basis, window_basis, ranks, inverses, child_map):
@@ -299,7 +299,7 @@
             pltpu.VMEM((512, 64), F32),
             pltpu.VMEM((8, 1024, 512), BF16),
             pltpu.VMEM((8, 64, 16, 64), BF16),
-            pltpu.VMEM((2, 512), I32),
+            pltpu.VMEM((2, 4096), I32),
             pltpu.SMEM((8, 16), I32),
             pltpu.VMEM((4, 8, 64, 128), BF16),
             pltpu.VMEM((16, 256, 128), BF16),
@@ -310,16 +310,15 @@
             pltpu.VMEM((64, 128), BF16),
             pltpu.VMEM((8, 64, 128), BF16),
             pltpu.VMEM((8, 2, 8, 512), BF16),
-            pltpu.VMEM((128, 512), BF16),
-            pltpu.VMEM((8, 64, 128), BF16),
-            pltpu.VMEM((576, 512), BF16),
-            pltpu.VMEM((2, 128, 128), BF16),
-            pltpu.VMEM((8, 16, 128), BF16),
-            pltpu.VMEM((8, 16, 128), BF16),
+            pltpu.VMEM((8, 2, 64, 512), BF16),
+            pltpu.VMEM((512, 128), F32),
+            pltpu.VMEM((2, 1024, 512), BF16),
+            pltpu.VMEM((8, 80, 128), BF16),
+            pltpu.VMEM((8, 80, 128), BF16),
             dma((6,)), dma((8,)), dma((7, 4)), dma((7, 4)),
             dma((8,)), dma((8,)),
             dma((8,)), dma((8,)), dma((8,)), dma((8,)),
-            dma((8,)), dma((8,)), dma((8,)), dma((8,)),
+            dma((8,)), dma((8,)), dma((7, 2)), dma((7, 2)),
         ],
         compiler_params=pltpu.CompilerParams(
             collective_id=0, has_side_effects=True, vmem_limit_bytes=56 * 1024 * 1024

time: 41.3 us -> 43.4 us (1.051)
  Pallas kernels: 39.1 us -> 41.4 us
    pallas_call x1, Pallas kernels: 39.1 us -> 41.4 us  [on_device(): pl.pallas_call(kernel, out_shape=(pltpu.VMEM((8, 2, 8, 64), BF16), pltpu....]
where the time goes in v3:
time: 43.4 us
  Pallas kernels  41.4 us (95%)
  local copies, waits for them, and re-layouts  1.31 us (3%)
  between operations  0.64 us (1%)
    pallas_call x1, Pallas kernels, on_device(): pl.pallas_call(kernel, out_shape=(pltpu.VMEM((8, 2, 8, 64), BF16), pltpu....  41.4 us

profile of v3, /device:TPU:1, one launch (start us, length us, event | category | flops | bytes accessed | tf_op | source)
XLA Modules:
  0.0 43.4 jit_solution(9328883454475793985)
XLA Ops:
  0.6 41.4 %shard_map.86 = (bf16[8,2,8,64]{3,2,1,0:T(8,128)(2,1)S(1)}, bf16[64,128]{1,0:T(8,128)(2,1)S(1)}) custom-call(f32[64,16,64]{2,1,0:T(8,128)} %right_ref.1, bf16[64,8,64]{2,1,0:T(8,128)(2,1)} %sol_ref.1, bf16[8,1024,512]{2,1,0:T(8,128)(2,1)} %basis_ref.1, bf16[8,64,16,64]{3,2,1,0:T(8,128)(2,1)} %wb_ref.1, s32[8,16]{1,0:T(8,128)} %ranks_ref.1, ...), custom_call_target="tpu_custom_call" | custom-call | flops 700000000 | bytes 12000000 | tf_op jit(solution)/shard_map/pallas_call | solution.py:287
  42.0 0.6 %copy.10 = bf16[64,16,8]{0,2,1:T(8,128)(2,1)} copy(bf16[64,16,8]{0,2,1:T(8,128)(2,1)S(1)} %bitcast.3) | data formatting | bytes 32768
  42.7 0.7 %reshape.11 = bf16[64,2,64]{2,1,0:T(2,128)(2,1)} reshape(bf16[64,128]{1,0:T(8,128)(2,1)S(1)} %get-tuple-element.5) | data formatting | bytes 32768 | tf_op jit(solution)/shard_map/reshape | solution.py:329

commit v4 on v2

--- a/solution.py
+++ b/solution.py
@@ -30,9 +30,9 @@
     right_ref, sol_ref, basis_ref, wb_ref, ranks_ref, inv_ref, map_ref,
     out_sol, out_child,
     sol_v, sol_f, right_v, right_f, basis_v, wb_v, map_v, ranks_s,
-    gath, w0, wt, cm, msg, part, red, redg, invg, invl, solg, selm, s5, pk, chg,
+    gath, half, w0, wt, cm, msg, part, red, redg, invg, invl, solg, selm, s5, pk, chg,
     load_sem, basis_sem, ring_send, ring_recv, inv_send, inv_recv,
-    p2_send, p2_recv, p3_send, p3_recv, p4_send, p4_recv, p5_send, p5_recv,
+    p2_send, p2_recv, p3_send, p3_recv, p4_send, p4_recv, p5_send, p5_recv, ready,
 ):
     r = lax.axis_index("row")
     c = lax.axis_index("col")
@@ -58,10 +58,22 @@
         inv_ref.at[pl.ds(2 * r, 2)], invg.at[r], load_sem, 5)
 
     barrier = pltpu.get_barrier_semaphore()
-    for d in NEAR:
-        pl.semaphore_signal(barrier, inc=1, device_id={"col": lax.rem(c + d, N)}, device_id_type=MESH)
-    for d in FAR_FIRST:
-        pl.semaphore_signal(barrier, inc=1, device_id={"row": lax.rem(r + d, N)}, device_id_type=MESH)
+
+    def lateness(axis, index):
+        return jnp.minimum(index, N - index) if axis == "col" else jnp.minimum(index // 2, 4 - index // 2)
+
+    peers = [("col", d) for d in NEAR] + [("row", d) for d in FAR_FIRST]
+    later, awaited = {}, 0
+    for axis, d in peers:
+        me = c if axis == "col" else r
+        to = lax.rem(me + d, N)
+        mine, its = lateness(axis, me), lateness(axis, to)
+        later[axis, d] = its > mine
+        awaited = awaited + jnp.where(its > mine, 0, 1)
+
+        @pl.when(its >= mine)
+        def _(axis=axis, to=to):
+            pl.semaphore_signal(barrier, inc=1, device_id={axis: to}, device_id_type=MESH)
 
     load_wb.start()
     load_map.start()
@@ -82,32 +94,50 @@
             [sol_f[pl.ds(2 * jj + h, 64, stride=8), :] for h in range(2)], axis=0)
         gath[jj, c] = both.T.astype(BF16)
 
-    pl.semaphore_wait(barrier, len(NEAR) + len(FAR_FIRST))
+    pl.semaphore_wait(barrier, awaited)
+    for n, (axis, d) in enumerate(peers):
+        me = c if axis == "col" else r
+        to = lax.rem(me + d, N)
+
+        @pl.when(lateness(axis, to) < lateness(axis, me))
+        def _(axis=axis, d=d, to=to):
+            pl.semaphore_signal(
+                ready.at[peers.index((axis, N - d))], inc=1, device_id={axis: to}, device_id_type=MESH)
+
+    def released(axis, d):
+        @pl.when(later[axis, d])
+        def _():
+            pl.semaphore_wait(ready.at[peers.index((axis, d))], 1)
 
     def chunk(jj, slot, to, lane):
         slot, to = lax.rem(c + slot + N, N), lax.rem(c + to + N, N)
         return remote(gath.at[jj, slot], gath.at[jj, slot], ring_send, ring_recv, (lane, jj), "col", to)
 
-    for jj in range(4):
-        chunk(jj, 0, 2, 0).start()
-        chunk(jj, 0, -2, 1).start()
-    for jj in range(4):
-        chunk(jj, 0, 1, 2).start()
-        chunk(jj, 0, -1, 3).start()
-
-    def relay(jj):
-        chunk(jj, -2, 2, 0).wait_recv()
-        if jj % 2 == 0:
-            chunk(jj, -2, 2, 6).start()
-        chunk(jj, -2, 1, 4).start()
-        chunk(jj, 2, -2, 1).wait_recv()
-        if jj % 2 == 1:
-            chunk(jj, 2, -2, 6).start()
-        chunk(jj, 2, -1, 5).start()
-
-    for d in FAR_FIRST:
-        to = lax.rem(r + d, N)
-        remote(inv_ref.at[pl.ds(2 * to, 2)], invg.at[r], inv_send, inv_recv, d, "row", to).start()
+    direct = ((2, 0), (-2, 1), (1, 2), (-1, 3))
+    for to, lane in direct:
+        @pl.when(jnp.logical_not(later["col", to % N]))
+        def _(to=to, lane=lane):
+            for jj in range(4):
+                chunk(jj, 0, to, lane).start()
+
+    for to, lane in direct:
+        @pl.when(later["col", to % N])
+        def _(to=to, lane=lane):
+            pl.semaphore_wait(ready.at[peers.index(("col", to % N))], 1)
+            for jj in range(4):
+                chunk(jj, 0, to, lane).start()
+
+    early = jnp.minimum(c, N - c) <= 1
+    halved = (c == 2) | (c == 6)
+
+    def relay(jj, side):
+        chunk(jj, -2 * side, 2 * side, (1 - side) // 2).wait_recv()
+
+        @pl.when(early | (halved if jj % 2 == (1 - side) // 2 else False))
+        def _():
+            chunk(jj, -2 * side, 2 * side, 6 + (1 - side) // 2).start()
+
+        chunk(jj, -2 * side, side, 4 + (1 - side) // 2).start()
 
     load_wb.wait()
     row_i, col_i = iota((256, 256), 0), iota((256, 256), 1)
@@ -124,12 +154,68 @@
 
     for step in range(16):
         regroup(step)
+    for first in (1, -1):
+        @pl.when((c < 4) if first == 1 else (c >= 4))
+        def _(first=first):
+            for side in (first, -first):
+                for jj in range(4):
+                    relay(jj, side)
+
+    for d in FAR_FIRST:
+        released("row", d)
+        to = lax.rem(r + d, N)
+        remote(inv_ref.at[pl.ds(2 * to, 2)], invg.at[r], inv_send, inv_recv, d, "row", to).start()
+
+    low = iota((1, 128), 1) < 64
+
+    def coeffs(jj, first):
+        pairs = [lax.rem(first + k, 4) for k in range(2)]
+        g = jnp.concatenate([gath[jj, pl.ds(2 * p, 2)].reshape(128, 128) for p in pairs], axis=0)
+        both = []
+        for h in range(2):
+            cols = [pl.ds(pl.multiple_of(p * 128, 128), 128) for p in pairs]
+            both.append(dot(jnp.concatenate([basis_v[2 * jj + h, :, at] for at in cols], axis=1), g))
+        return jnp.where(low, both[0], both[1])
+
+    near = lax.rem((c + 7) // 2, 4)
     for jj in range(4):
-        relay(jj)
+        chunk(jj, 0, 1, 2).wait_recv()
+        chunk(jj, 0, 1, 3).wait_recv()
+        loads[2 * jj].wait()
+        loads[2 * jj + 1].wait()
+        half[jj] = coeffs(jj, near)
     for i in range(16):
         wt[i] = w0[i].T
-
-    low = iota((1, 128), 1) < 64
+    load_ranks.wait()
+
+    k_of = iota((64, 128), 0)
+    for jj in range(4):
+        over = jnp.where(lax.rem(c, 4) == 0, jj % 2, c // 4)
+        for lane in (4, 5, 6 + over):
+            chunk(jj, 0, 1, lane).wait_recv()
+        total = half[jj] + coeffs(jj, lax.rem(near + 2, 4))
+        for i in range(16):
+            limit = jnp.where(low, ranks_s[2 * jj, i], ranks_s[2 * jj + 1, i])
+            cut = jnp.where(k_of < limit, total[i * 64:(i + 1) * 64], 0.0)
+            cm[i, jj * 64:(jj + 1) * 64, :] = cut.astype(BF16)
+
+    def update(to):
+        sums = []
+        for h in range(2):
+            u = dot(wt[2 * to + h], cm[2 * to + h])
+            sums.append(jnp.where(low, u[0:64], u[64:128]))
+        return jnp.where(low, sums[0], sums[1]) + swap(jnp.where(low, sums[1], sums[0]))
+
+    def p2(d, to):
+        return remote(msg.at[d], part.at[d], p2_send, p2_recv, d, "row", to)
+
+    for batch in (FAR_FIRST[:4], FAR_FIRST[4:]):
+        for d in batch:
+            msg[d] = update(lax.rem(r + d, N)).astype(BF16)
+        for d in batch:
+            p2(d, lax.rem(r + d, N)).start()
+    own_update = update(r)
+
     load_map.wait()
     w = map_v[...]
     cc = (w >> 3) & 7
@@ -161,6 +247,30 @@
     selm[512:576, :] = jnp.where(
         la == ((ra >> 3) << 6) + r * 8 + (ra & 7), 1.0, 0.0).astype(BF16)
 
+    load_right.wait()
+    right_f[...] = right_v[...].reshape(512, 64)
+    base = 2 * lax.rem(r, 4)
+    right_t = jnp.concatenate(
+        [right_f[pl.ds(base + h, 64, stride=8), :] for h in range(2)], axis=0).T
+
+    acc = right_t - own_update
+    for d in range(1, N):
+        p2(d, r).wait_recv()
+        acc = acc - part[d].astype(F32)
+    red[...] = acc.astype(BF16)
+    redg[c] = acc.astype(BF16)
+
+    def p3(d, to):
+        return remote(red, redg.at[c], p3_send, p3_recv, d, "col", to)
+
+    for d in FAR_FIRST:
+        p3(d, lax.rem(c + d, N)).start()
+    load_inv.wait()
+    for d in range(1, N):
+        remote(inv_ref.at[pl.ds(2 * r, 2)], invg.at[r], inv_send, inv_recv, d, "row", r).wait_recv()
+    for h in range(2):
+        invl[h * 64:(h + 1) * 64, :] = invg[:, h].astype(F32).reshape(64, 512).astype(BF16)
+
     x = map_v[:, pl.ds(pl.multiple_of((c // 2) * 128, 128), 128)]
     x_swapped = swap(x)
     odd = lax.rem(c, 2) == 1
@@ -175,62 +285,6 @@
     for h in range(2):
         s5[h] = jnp.where((qb == found) & ((rank_i >> 4) == h), 1.0, 0.0).astype(BF16)
 
-    load_right.wait()
-    right_f[...] = right_v[...].reshape(512, 64)
-    base = 2 * lax.rem(r, 4)
-    right_t = jnp.concatenate(
-        [right_f[pl.ds(base + h, 64, stride=8), :] for h in range(2)], axis=0).T
-
-    load_ranks.wait()
-
-    k_of = iota((64, 128), 0)
-    for jj in range(4):
-        for lane in (2, 3, 4, 5, 6):
-            chunk(jj, 0, 1, lane).wait_recv()
-        loads[2 * jj].wait()
-        loads[2 * jj + 1].wait()
-        g = gath[jj].reshape(512, 128)
-        pair = [dot(basis_v[2 * jj + h], g) for h in range(2)]
-        for i in range(16):
-            at = slice(i * 64, (i + 1) * 64)
-            limit = jnp.where(low, ranks_s[2 * jj, i], ranks_s[2 * jj + 1, i])
-            both = jnp.where(low, pair[0][at], pair[1][at])
-            cm[i, jj * 64:(jj + 1) * 64, :] = jnp.where(k_of < limit, both, 0.0).astype(BF16)
-
-    def update(to):
-        sums = []
-        for h in range(2):
-            u = dot(wt[2 * to + h], cm[2 * to + h])
-            sums.append(jnp.where(low, u[0:64], u[64:128]))
-        return jnp.where(low, sums[0], sums[1]) + swap(jnp.where(low, sums[1], sums[0]))
-
-    def p2(d, to):
-        return remote(msg.at[d], part.at[d], p2_send, p2_recv, d, "row", to)
-
-    for batch in (FAR_FIRST[:4], FAR_FIRST[4:]):
-        for d in batch:
-            msg[d] = update(lax.rem(r + d, N)).astype(BF16)
-        for d in batch:
-            p2(d, lax.rem(r + d, N)).start()
-    acc = right_t - update(r)
-
-    load_inv.wait()
-    for d in range(1, N):
-        remote(inv_ref.at[pl.ds(2 * r, 2)], invg.at[r], inv_send, inv_recv, d, "row", r).wait_recv()
-    for h in range(2):
-        invl[h * 64:(h + 1) * 64, :] = invg[:, h].astype(F32).reshape(64, 512).astype(BF16)
-
-    for d in range(1, N):
-        p2(d, r).wait_recv()
-        acc = acc - part[d].astype(F32)
-    red[...] = acc.astype(BF16)
-    redg[c] = acc.astype(BF16)
-
-    def p3(d, to):
-        return remote(red, redg.at[c], p3_send, p3_recv, d, "col", to)
-
-    for d in FAR_FIRST:
-        p3(d, lax.rem(c + d, N)).start()
     for d in range(1, N):
         p3(d, c).wait_recv()
 
@@ -270,8 +324,12 @@
     out_child[...] = child.T[0:64].astype(BF16)
 
     for jj in range(4):
-        for lane in range(7):
+        for lane in range(6):
             chunk(jj, 0, 1, lane).wait_send()
+        for lane in (6, 7):
+            @pl.when(early | (halved if jj % 2 == lane - 6 else False))
+            def _(jj=jj, lane=lane):
+                chunk(jj, 0, 1, lane).wait_send()
     for d in range(1, N):
         remote(inv_ref.at[pl.ds(2 * r, 2)], invg.at[r], inv_send, inv_recv, d, "row", r).wait_send()
         p2(d, r).wait_send()
@@ -302,6 +360,7 @@
             pltpu.VMEM((2, 512), I32),
             pltpu.SMEM((8, 16), I32),
             pltpu.VMEM((4, 8, 64, 128), BF16),
+            pltpu.VMEM((4, 1024, 128), F32),
             pltpu.VMEM((16, 256, 128), BF16),
             pltpu.VMEM((16, 128, 256), BF16),
             pltpu.VMEM((16, 256, 128), BF16),
@@ -316,10 +375,11 @@
             pltpu.VMEM((2, 128, 128), BF16),
             pltpu.VMEM((8, 16, 128), BF16),
             pltpu.VMEM((8, 16, 128), BF16),
-            dma((6,)), dma((8,)), dma((7, 4)), dma((7, 4)),
+            dma((6,)), dma((8,)), dma((8, 4)), dma((8, 4)),
             dma((8,)), dma((8,)),
             dma((8,)), dma((8,)), dma((8,)), dma((8,)),
             dma((8,)), dma((8,)), dma((8,)), dma((8,)),
+            pltpu.SemaphoreType.REGULAR((len(NEAR) + len(FAR_FIRST),)),
         ],
         compiler_params=pltpu.CompilerParams(
             collective_id=0, has_side_effects=True, vmem_limit_bytes=56 * 1024 * 1024

time: 41.3 us -> 42 us (1.017)
  Pallas kernels: 39.1 us -> 39.9 us
    pallas_call x1, Pallas kernels: 39.1 us -> 39.9 us  [on_device(): pl.pallas_call(kernel, out_shape=(pltpu.VMEM((8, 2, 8, 64), BF16), pltpu....]
where the time goes in v4:
time: 42 us; the launch traced here: 41.8 us
  Pallas kernels  39.9 us (95%)
  local copies, waits for them, and re-layouts  1.31 us (3%)
  between operations  0.64 us (2%)
    pallas_call x1, Pallas kernels, on_device(): pl.pallas_call(kernel, out_shape=(pltpu.VMEM((8, 2, 8, 64), BF16), pltpu....  39.9 us

profile of v4, /device:TPU:1, one launch (start us, length us, event | category | flops | bytes accessed | tf_op | source)
XLA Modules:
  0.0 41.8 jit_solution(5585871616857897698)
XLA Ops:
  0.6 39.9 %shard_map.86 = (bf16[8,2,8,64]{3,2,1,0:T(8,128)(2,1)S(1)}, bf16[64,128]{1,0:T(8,128)(2,1)S(1)}) custom-call(f32[64,16,64]{2,1,0:T(8,128)} %right_ref.1, bf16[64,8,64]{2,1,0:T(8,128)(2,1)} %sol_ref.1, bf16[8,1024,512]{2,1,0:T(8,128)(2,1)} %basis_ref.1, bf16[8,64,16,64]{3,2,1,0:T(8,128)(2,1)} %wb_ref.1, s32[8,16]{1,0:T(8,128)} %ranks_ref.1, ...), custom_call_target="tpu_custom_call" | custom-call | flops 700000000 | bytes 12000000 | tf_op jit(solution)/shard_map/pallas_call | solution.py:345
  40.5 0.6 %copy.10 = bf16[64,16,8]{0,2,1:T(8,128)(2,1)} copy(bf16[64,16,8]{0,2,1:T(8,128)(2,1)S(1)} %bitcast.3) | data formatting | bytes 32768
  41.1 0.7 %reshape.11 = bf16[64,2,64]{2,1,0:T(2,128)(2,1)} reshape(bf16[64,128]{1,0:T(8,128)(2,1)S(1)} %get-tuple-element.5) | data formatting | bytes 32768 | tf_op jit(solution)/shard_map/reshape | solution.py:390

commit v5 on v4

--- a/solution.py
+++ b/solution.py
@@ -32,7 +32,7 @@
     sol_v, sol_f, right_v, right_f, basis_v, wb_v, map_v, ranks_s,
     gath, half, w0, wt, cm, msg, part, red, redg, invg, invl, solg, selm, s5, pk, chg,
     load_sem, basis_sem, ring_send, ring_recv, inv_send, inv_recv,
-    p2_send, p2_recv, p3_send, p3_recv, p4_send, p4_recv, p5_send, p5_recv, ready,
+    p2_send, p2_recv, p3_send, p3_recv, p4_send, p4_recv, p5_send, p5_recv,
 ):
     r = lax.axis_index("row")
     c = lax.axis_index("col")
@@ -58,34 +58,30 @@
         inv_ref.at[pl.ds(2 * r, 2)], invg.at[r], load_sem, 5)
 
     barrier = pltpu.get_barrier_semaphore()
-
-    def lateness(axis, index):
-        return jnp.minimum(index, N - index) if axis == "col" else jnp.minimum(index // 2, 4 - index // 2)
-
-    peers = [("col", d) for d in NEAR] + [("row", d) for d in FAR_FIRST]
-    later, awaited = {}, 0
-    for axis, d in peers:
-        me = c if axis == "col" else r
-        to = lax.rem(me + d, N)
-        mine, its = lateness(axis, me), lateness(axis, to)
-        later[axis, d] = its > mine
-        awaited = awaited + jnp.where(its > mine, 0, 1)
-
-        @pl.when(its >= mine)
-        def _(axis=axis, to=to):
-            pl.semaphore_signal(barrier, inc=1, device_id={axis: to}, device_id_type=MESH)
+    for d in NEAR:
+        pl.semaphore_signal(barrier, inc=1, device_id={"col": lax.rem(c + d, N)}, device_id_type=MESH)
+    for d in FAR_FIRST:
+        pl.semaphore_signal(barrier, inc=1, device_id={"row": lax.rem(r + d, N)}, device_id_type=MESH)
+
+    def loop(count, body):
+        def step(n, carry):
+            body(n)
+            return carry
+
+        lax.fori_loop(0, count, step, 0)
+
+    def away(n):
+        return 4 + (n + 1) // 2 * (1 - 2 * lax.rem(n, 2))
 
     load_wb.start()
     load_map.start()
     load_ranks.start()
     load_right.start()
     load_inv.start()
-    loads = [
-        local(basis_ref.at[j], basis_v.at[j], basis_sem, j)
-        for j in range(N)
-    ]
-    for load in loads:
-        load.start()
+    def load_basis(j):
+        return local(basis_ref.at[j], basis_v.at[j], basis_sem, j)
+
+    loop(N, lambda j: load_basis(j).start())
 
     load_sol.wait()
     sol_f[...] = sol_v[...].astype(F32).reshape(512, 64)
@@ -94,50 +90,38 @@
             [sol_f[pl.ds(2 * jj + h, 64, stride=8), :] for h in range(2)], axis=0)
         gath[jj, c] = both.T.astype(BF16)
 
-    pl.semaphore_wait(barrier, awaited)
-    for n, (axis, d) in enumerate(peers):
-        me = c if axis == "col" else r
-        to = lax.rem(me + d, N)
-
-        @pl.when(lateness(axis, to) < lateness(axis, me))
-        def _(axis=axis, d=d, to=to):
-            pl.semaphore_signal(
-                ready.at[peers.index((axis, N - d))], inc=1, device_id={axis: to}, device_id_type=MESH)
-
-    def released(axis, d):
-        @pl.when(later[axis, d])
-        def _():
-            pl.semaphore_wait(ready.at[peers.index((axis, d))], 1)
+    pl.semaphore_wait(barrier, len(NEAR) + len(FAR_FIRST))
 
     def chunk(jj, slot, to, lane):
         slot, to = lax.rem(c + slot + N, N), lax.rem(c + to + N, N)
         return remote(gath.at[jj, slot], gath.at[jj, slot], ring_send, ring_recv, (lane, jj), "col", to)
 
-    direct = ((2, 0), (-2, 1), (1, 2), (-1, 3))
-    for to, lane in direct:
-        @pl.when(jnp.logical_not(later["col", to % N]))
-        def _(to=to, lane=lane):
-            for jj in range(4):
-                chunk(jj, 0, to, lane).start()
-
-    for to, lane in direct:
-        @pl.when(later["col", to % N])
-        def _(to=to, lane=lane):
-            pl.semaphore_wait(ready.at[peers.index(("col", to % N))], 1)
-            for jj in range(4):
-                chunk(jj, 0, to, lane).start()
-
-    early = jnp.minimum(c, N - c) <= 1
-    halved = (c == 2) | (c == 6)
-
-    def relay(jj, side):
-        chunk(jj, -2 * side, 2 * side, (1 - side) // 2).wait_recv()
-
-        @pl.when(early | (halved if jj % 2 == (1 - side) // 2 else False))
-        def _():
-            chunk(jj, -2 * side, 2 * side, 6 + (1 - side) // 2).start()
-
-        chunk(jj, -2 * side, side, 4 + (1 - side) // 2).start()
+    def direct(jj):
+        chunk(jj, 0, 2, 0).start()
+        chunk(jj, 0, -2, 1).start()
+
+    def next_to(jj):
+        chunk(jj, 0, 1, 2).start()
+        chunk(jj, 0, -1, 3).start()
+
+    loop(4, direct)
+    loop(4, next_to)
+
+    def tile_rows(d, to):
+        return remote(inv_ref.at[pl.ds(2 * to, 2)], invg.at[r], inv_send, inv_recv, d, "row", to)
+
+    loop(N - 1, lambda n: tile_rows(away(n), lax.rem(r + away(n), N)).start())
+
+    def relay(jj):
+        way = 1 - 2 * lax.rem(jj, 2)
+        for side in (1, -1):
+            chunk(jj, -2 * side, 2 * side, (1 - side) // 2).wait_recv()
+
+            @pl.when(way == side)
+            def _(side=side):
+                chunk(jj, -2 * side, 2 * side, 6).start()
+
+            chunk(jj, -2 * side, side, 4 + (1 - side) // 2).start()
 
     load_wb.wait()
     row_i, col_i = iota((256, 256), 0), iota((256, 256), 1)
@@ -145,26 +129,15 @@
         ((row_i >> 4) == (col_i & 15)) & ((row_i & 15) == (col_i >> 4)), 1.0, 0.0).astype(BF16)
 
     def regroup(step):
-        jj, kb = step // 4, step % 4
+        jj, kb = step // 4, lax.rem(step, 4)
         k0 = pl.multiple_of(kb * 16, 16)
         x = jnp.concatenate(
             [wb_v[2 * jj + h, pl.ds(k0, 16)].reshape(256, 64) for h in range(2)], axis=1)
         y = dot(perm, x).astype(BF16).reshape(16, 16, 128)
         w0[:, pl.ds(pl.multiple_of(jj * 64 + kb * 16, 16), 16), :] = y
 
-    for step in range(16):
-        regroup(step)
-    for first in (1, -1):
-        @pl.when((c < 4) if first == 1 else (c >= 4))
-        def _(first=first):
-            for side in (first, -first):
-                for jj in range(4):
-                    relay(jj, side)
-
-    for d in FAR_FIRST:
-        released("row", d)
-        to = lax.rem(r + d, N)
-        remote(inv_ref.at[pl.ds(2 * to, 2)], invg.at[r], inv_send, inv_recv, d, "row", to).start()
+    loop(16, regroup)
+    loop(4, relay)
 
     low = iota((1, 128), 1) < 64
 
@@ -178,26 +151,33 @@
         return jnp.where(low, both[0], both[1])
 
     near = lax.rem((c + 7) // 2, 4)
-    for jj in range(4):
+
+    def near_half(jj):
         chunk(jj, 0, 1, 2).wait_recv()
         chunk(jj, 0, 1, 3).wait_recv()
-        loads[2 * jj].wait()
-        loads[2 * jj + 1].wait()
+        load_basis(2 * jj).wait()
+        load_basis(2 * jj + 1).wait()
         half[jj] = coeffs(jj, near)
-    for i in range(16):
+
+    loop(4, near_half)
+
+    def turn(i):
         wt[i] = w0[i].T
+
+    loop(16, turn)
     load_ranks.wait()
-
     k_of = iota((64, 128), 0)
-    for jj in range(4):
-        over = jnp.where(lax.rem(c, 4) == 0, jj % 2, c // 4)
-        for lane in (4, 5, 6 + over):
+
+    def far_half(jj):
+        for lane in (4, 5, 6):
             chunk(jj, 0, 1, lane).wait_recv()
         total = half[jj] + coeffs(jj, lax.rem(near + 2, 4))
         for i in range(16):
             limit = jnp.where(low, ranks_s[2 * jj, i], ranks_s[2 * jj + 1, i])
             cut = jnp.where(k_of < limit, total[i * 64:(i + 1) * 64], 0.0)
-            cm[i, jj * 64:(jj + 1) * 64, :] = cut.astype(BF16)
+            cm[i, pl.ds(pl.multiple_of(jj * 64, 64), 64), :] = cut.astype(BF16)
+
+    loop(4, far_half)
 
     def update(to):
         sums = []
@@ -209,11 +189,13 @@
     def p2(d, to):
         return remote(msg.at[d], part.at[d], p2_send, p2_recv, d, "row", to)
 
-    for batch in (FAR_FIRST[:4], FAR_FIRST[4:]):
-        for d in batch:
-            msg[d] = update(lax.rem(r + d, N)).astype(BF16)
-        for d in batch:
-            p2(d, lax.rem(r + d, N)).start()
+    def send_update(n):
+        d = away(n)
+        to = lax.rem(r + d, N)
+        msg[d] = update(to).astype(BF16)
+        p2(d, to).start()
+
+    loop(N - 1, send_update)
     own_update = update(r)
 
     load_map.wait()
@@ -254,20 +236,20 @@
         [right_f[pl.ds(base + h, 64, stride=8), :] for h in range(2)], axis=0).T
 
     acc = right_t - own_update
-    for d in range(1, N):
-        p2(d, r).wait_recv()
-        acc = acc - part[d].astype(F32)
+    def less(n, acc):
+        p2(n + 1, r).wait_recv()
+        return acc - part[n + 1].astype(F32)
+
+    acc = lax.fori_loop(0, N - 1, less, acc)
     red[...] = acc.astype(BF16)
     redg[c] = acc.astype(BF16)
 
     def p3(d, to):
         return remote(red, redg.at[c], p3_send, p3_recv, d, "col", to)
 
-    for d in FAR_FIRST:
-        p3(d, lax.rem(c + d, N)).start()
+    loop(N - 1, lambda n: p3(away(n), lax.rem(c + away(n), N)).start())
     load_inv.wait()
-    for d in range(1, N):
-        remote(inv_ref.at[pl.ds(2 * r, 2)], invg.at[r], inv_send, inv_recv, d, "row", r).wait_recv()
+    loop(N - 1, lambda n: tile_rows(n + 1, r).wait_recv())
     for h in range(2):
         invl[h * 64:(h + 1) * 64, :] = invg[:, h].astype(F32).reshape(64, 512).astype(BF16)
 
@@ -285,8 +267,7 @@
     for h in range(2):
         s5[h] = jnp.where((qb == found) & ((rank_i >> 4) == h), 1.0, 0.0).astype(BF16)
 
-    for d in range(1, N):
-        p3(d, c).wait_recv()
+    loop(N - 1, lambda n: p3(n + 1, c).wait_recv())
 
     s = dot(invl[...], redg[...].reshape(512, 128))
     solved = jnp.where(low, s[0:64], s[64:128]).astype(BF16)
@@ -295,10 +276,8 @@
     def p4(d, to):
         return remote(solg.at[r], solg.at[r], p4_send, p4_recv, d, "row", to)
 
-    for d in FAR_FIRST:
-        p4(d, lax.rem(r + d, N)).start()
-    for d in range(1, N):
-        p4(d, r).wait_recv()
+    loop(N - 1, lambda n: p4(away(n), lax.rem(r + away(n), N)).start())
+    loop(N - 1, lambda n: p4(n + 1, r).wait_recv())
 
     picked = dot(selm[...], solg[...].reshape(512, 128))
     rows = jnp.where(low, picked[0:256], picked[256:512])
@@ -309,33 +288,31 @@
     def p5(d, to):
         return remote(pk.at[to], chg.at[c], p5_send, p5_recv, d, "col", to)
 
-    for d in FAR_FIRST:
-        p5(d, lax.rem(c + d, N)).start()
+    loop(N - 1, lambda n: p5(away(n), lax.rem(c + away(n), N)).start())
 
     own_rows = picked[512:576]
     out_sol[:, 0] = own_rows[:, 0:64].reshape(8, 8, 64).astype(BF16)
     out_sol[:, 1] = swap(own_rows)[:, 0:64].reshape(8, 8, 64).astype(BF16)
 
-    for d in range(1, N):
-        p5(d, c).wait_recv()
+    loop(N - 1, lambda n: p5(n + 1, c).wait_recv())
     got = chg[...].reshape(128, 128)
     child = jnp.where(low, dot(s5[0], got), dot(s5[1], got))
     child = child + swap(child)
     out_child[...] = child.T[0:64].astype(BF16)
 
-    for jj in range(4):
-        for lane in range(6):
-            chunk(jj, 0, 1, lane).wait_send()
-        for lane in (6, 7):
-            @pl.when(early | (halved if jj % 2 == lane - 6 else False))
-            def _(jj=jj, lane=lane):
-                chunk(jj, 0, 1, lane).wait_send()
-    for d in range(1, N):
-        remote(inv_ref.at[pl.ds(2 * r, 2)], invg.at[r], inv_send, inv_recv, d, "row", r).wait_send()
-        p2(d, r).wait_send()
-        p3(d, c).wait_send()
-        p4(d, r).wait_send()
-        p5(d, c).wait_send()
+    def sent(n):
+        chunk(n // 7, 0, 1, lax.rem(n, 7)).wait_send()
+
+    loop(28, sent)
+
+    def sent_rows(n):
+        tile_rows(n + 1, r).wait_send()
+        p2(n + 1, r).wait_send()
+        p3(n + 1, c).wait_send()
+        p4(n + 1, r).wait_send()
+        p5(n + 1, c).wait_send()
+
+    loop(N - 1, sent_rows)
 
 
 def on_device(right_side, rest_solution, rest_basis, window_basis, ranks, inverses, child_map):
@@ -375,11 +352,10 @@
             pltpu.VMEM((2, 128, 128), BF16),
             pltpu.VMEM((8, 16, 128), BF16),
             pltpu.VMEM((8, 16, 128), BF16),
-            dma((6,)), dma((8,)), dma((8, 4)), dma((8, 4)),
+            dma((6,)), dma((8,)), dma((7, 4)), dma((7, 4)),
             dma((8,)), dma((8,)),
             dma((8,)), dma((8,)), dma((8,)), dma((8,)),
             dma((8,)), dma((8,)), dma((8,)), dma((8,)),
-            pltpu.SemaphoreType.REGULAR((len(NEAR) + len(FAR_FIRST),)),
         ],
         compiler_params=pltpu.CompilerParams(
             collective_id=0, has_side_effects=True, vmem_limit_bytes=56 * 1024 * 1024

time: 42 us -> 41.8 us (level)
  no operation moved by 1% of the time
where the time goes in v5:
time: 41.8 us; the launch traced here: 41.4 us
  Pallas kernels  39.5 us (94%)
  local copies, waits for them, and re-layouts  1.31 us (3%)
  between operations  0.64 us (2%)
    pallas_call x1, Pallas kernels, on_device(): pl.pallas_call(kernel, out_shape=(pltpu.VMEM((8, 2, 8, 64), BF16), pltpu....  39.5 us

profile of v5, /device:TPU:1, one launch (start us, length us, event | category | flops | bytes accessed | tf_op | source)
XLA Modules:
  0.0 41.4 jit_solution(9289210982124143283)
XLA Ops:
  0.6 39.5 %shard_map.86 = (bf16[8,2,8,64]{3,2,1,0:T(8,128)(2,1)S(1)}, bf16[64,128]{1,0:T(8,128)(2,1)S(1)}) custom-call(f32[64,16,64]{2,1,0:T(8,128)} %right_ref.1, bf16[64,8,64]{2,1,0:T(8,128)(2,1)} %sol_ref.1, bf16[8,1024,512]{2,1,0:T(8,128)(2,1)} %basis_ref.1, bf16[8,64,16,64]{3,2,1,0:T(8,128)(2,1)} %wb_ref.1, s32[8,16]{1,0:T(8,128)} %ranks_ref.1, ...), custom_call_target="tpu_custom_call" | custom-call | flops 700000000 | bytes 12000000 | tf_op jit(solution)/shard_map/pallas_call | solution.py:322
  40.1 0.6 %copy.10 = bf16[64,16,8]{0,2,1:T(8,128)(2,1)} copy(bf16[64,16,8]{0,2,1:T(8,128)(2,1)S(1)} %bitcast.3) | data formatting | bytes 32768
  40.7 0.7 %reshape.11 = bf16[64,2,64]{2,1,0:T(2,128)(2,1)} reshape(bf16[64,128]{1,0:T(8,128)(2,1)S(1)} %get-tuple-element.5) | data formatting | bytes 32768 | tf_op jit(solution)/shard_map/reshape | solution.py:366

commit v6 on v5

--- a/solution.py
+++ b/solution.py
@@ -70,6 +70,10 @@
 
         lax.fori_loop(0, count, step, 0)
 
+    def all_seven(ref, sem):
+        seven = ref.at[pl.ds(0, N - 1)]
+        pltpu.make_async_copy(seven, seven, sem.at[0]).wait()
+
     def away(n):
         return 4 + (n + 1) // 2 * (1 - 2 * lax.rem(n, 2))
 
@@ -108,7 +112,7 @@
     loop(4, next_to)
 
     def tile_rows(d, to):
-        return remote(inv_ref.at[pl.ds(2 * to, 2)], invg.at[r], inv_send, inv_recv, d, "row", to)
+        return remote(inv_ref.at[pl.ds(2 * to, 2)], invg.at[r], inv_send, inv_recv, 0, "row", to)
 
     loop(N - 1, lambda n: tile_rows(away(n), lax.rem(r + away(n), N)).start())
 
@@ -187,7 +191,7 @@
         return jnp.where(low, sums[0], sums[1]) + swap(jnp.where(low, sums[1], sums[0]))
 
     def p2(d, to):
-        return remote(msg.at[d], part.at[d], p2_send, p2_recv, d, "row", to)
+        return remote(msg.at[d], part.at[d], p2_send, p2_recv, 0, "row", to)
 
     def send_update(n):
         d = away(n)
@@ -236,20 +240,18 @@
         [right_f[pl.ds(base + h, 64, stride=8), :] for h in range(2)], axis=0).T
 
     acc = right_t - own_update
-    def less(n, acc):
-        p2(n + 1, r).wait_recv()
-        return acc - part[n + 1].astype(F32)
-
-    acc = lax.fori_loop(0, N - 1, less, acc)
+    all_seven(part, p2_recv)
+    for d in range(1, N):
+        acc = acc - part[d].astype(F32)
     red[...] = acc.astype(BF16)
     redg[c] = acc.astype(BF16)
 
     def p3(d, to):
-        return remote(red, redg.at[c], p3_send, p3_recv, d, "col", to)
+        return remote(red, redg.at[c], p3_send, p3_recv, 0, "col", to)
 
     loop(N - 1, lambda n: p3(away(n), lax.rem(c + away(n), N)).start())
     load_inv.wait()
-    loop(N - 1, lambda n: tile_rows(n + 1, r).wait_recv())
+    all_seven(invg, inv_recv)
     for h in range(2):
         invl[h * 64:(h + 1) * 64, :] = invg[:, h].astype(F32).reshape(64, 512).astype(BF16)
 
@@ -267,17 +269,17 @@
     for h in range(2):
         s5[h] = jnp.where((qb == found) & ((rank_i >> 4) == h), 1.0, 0.0).astype(BF16)
 
-    loop(N - 1, lambda n: p3(n + 1, c).wait_recv())
+    all_seven(redg, p3_recv)
 
     s = dot(invl[...], redg[...].reshape(512, 128))
     solved = jnp.where(low, s[0:64], s[64:128]).astype(BF16)
     solg[r] = solved
 
     def p4(d, to):
-        return remote(solg.at[r], solg.at[r], p4_send, p4_recv, d, "row", to)
+        return remote(solg.at[r], solg.at[r], p4_send, p4_recv, 0, "row", to)
 
     loop(N - 1, lambda n: p4(away(n), lax.rem(r + away(n), N)).start())
-    loop(N - 1, lambda n: p4(n + 1, r).wait_recv())
+    all_seven(solg, p4_recv)
 
     picked = dot(selm[...], solg[...].reshape(512, 128))
     rows = jnp.where(low, picked[0:256], picked[256:512])
@@ -286,7 +288,7 @@
     chg[c] = pk[c]
 
     def p5(d, to):
-        return remote(pk.at[to], chg.at[c], p5_send, p5_recv, d, "col", to)
+        return remote(pk.at[to], chg.at[c], p5_send, p5_recv, 0, "col", to)
 
     loop(N - 1, lambda n: p5(away(n), lax.rem(c + away(n), N)).start())
 
@@ -294,25 +296,21 @@
     out_sol[:, 0] = own_rows[:, 0:64].reshape(8, 8, 64).astype(BF16)
     out_sol[:, 1] = swap(own_rows)[:, 0:64].reshape(8, 8, 64).astype(BF16)
 
-    loop(N - 1, lambda n: p5(n + 1, c).wait_recv())
+    def sent(n):
+        chunk(n // 7, 0, 1, lax.rem(n, 7)).wait_send()
+
+    loop(28, sent)
+    all_seven(invg, inv_send)
+    all_seven(msg, p2_send)
+    all_seven(redg, p3_send)
+    all_seven(solg, p4_send)
+
+    all_seven(chg, p5_recv)
     got = chg[...].reshape(128, 128)
     child = jnp.where(low, dot(s5[0], got), dot(s5[1], got))
     child = child + swap(child)
     out_child[...] = child.T[0:64].astype(BF16)
-
-    def sent(n):
-        chunk(n // 7, 0, 1, lax.rem(n, 7)).wait_send()
-
-    loop(28, sent)
-
-    def sent_rows(n):
-        tile_rows(n + 1, r).wait_send()
-        p2(n + 1, r).wait_send()
-        p3(n + 1, c).wait_send()
-        p4(n + 1, r).wait_send()
-        p5(n + 1, c).wait_send()
-
-    loop(N - 1, sent_rows)
+    all_seven(pk, p5_send)
 
 
 def on_device(right_side, rest_solution, rest_basis, window_basis, ranks, inverses, child_map):
@@ -353,9 +351,9 @@
             pltpu.VMEM((8, 16, 128), BF16),
             pltpu.VMEM((8, 16, 128), BF16),
             dma((6,)), dma((8,)), dma((7, 4)), dma((7, 4)),
-            dma((8,)), dma((8,)),
-            dma((8,)), dma((8,)), dma((8,)), dma((8,)),
-            dma((8,)), dma((8,)), dma((8,)), dma((8,)),
+            dma((1,)), dma((1,)),
+            dma((1,)), dma((1,)), dma((1,)), dma((1,)),
+            dma((1,)), dma((1,)), dma((1,)), dma((1,)),
         ],
         compiler_params=pltpu.CompilerParams(
             collective_id=0, has_side_effects=True, vmem_limit_bytes=56 * 1024 * 1024

time: 41.8 us -> 40.6 us (0.971)
  Pallas kernels: 39.5 us -> 38.3 us
    pallas_call x1, Pallas kernels: 39.5 us -> 38.3 us  [on_device(): pl.pallas_call(kernel, out_shape=(pltpu.VMEM((8, 2, 8, 64), BF16), pltpu....]
where the time goes in v6:
time: 40.6 us; the launch traced here: 40.3 us
  Pallas kernels  38.3 us (94%)
  local copies, waits for them, and re-layouts  1.31 us (3%)
  between operations  0.64 us (2%)
    pallas_call x1, Pallas kernels, on_device(): pl.pallas_call(kernel, out_shape=(pltpu.VMEM((8, 2, 8, 64), BF16), pltpu....  38.3 us

profile of v6, /device:TPU:1, one launch (start us, length us, event | category | flops | bytes accessed | tf_op | source)
XLA Modules:
  0.0 40.3 jit_solution(538034741380557111)
XLA Ops:
  0.6 38.3 %shard_map.86 = (bf16[8,2,8,64]{3,2,1,0:T(8,128)(2,1)S(1)}, bf16[64,128]{1,0:T(8,128)(2,1)S(1)}) custom-call(f32[64,16,64]{2,1,0:T(8,128)} %right_ref.1, bf16[64,8,64]{2,1,0:T(8,128)(2,1)} %sol_ref.1, bf16[8,1024,512]{2,1,0:T(8,128)(2,1)} %basis_ref.1, bf16[8,64,16,64]{3,2,1,0:T(8,128)(2,1)} %wb_ref.1, s32[8,16]{1,0:T(8,128)} %ranks_ref.1, ...), custom_call_target="tpu_custom_call" | custom-call | flops 700000000 | bytes 12000000 | tf_op jit(solution)/shard_map/pallas_call | solution.py:320
  39.0 0.6 %copy.10 = bf16[64,16,8]{0,2,1:T(8,128)(2,1)} copy(bf16[64,16,8]{0,2,1:T(8,128)(2,1)S(1)} %bitcast.3) | data formatting | bytes 32768
  39.6 0.7 %reshape.11 = bf16[64,2,64]{2,1,0:T(2,128)(2,1)} reshape(bf16[64,128]{1,0:T(8,128)(2,1)S(1)} %get-tuple-element.5) | data formatting | bytes 32768 | tf_op jit(solution)/shard_map/reshape | solution.py:364

commit v7 on v6

--- a/solution.py
+++ b/solution.py
@@ -140,7 +140,20 @@
         y = dot(perm, x).astype(BF16).reshape(16, 16, 128)
         w0[:, pl.ds(pl.multiple_of(jj * 64 + kb * 16, 16), 16), :] = y
 
-    loop(16, regroup)
+    def regroups(n):
+        for k in range(4):
+            regroup(4 * n + k)
+
+    loop(4, regroups)
+
+    def turn(i):
+        wt[i] = w0[i].T
+
+    def turns(n):
+        for k in range(4):
+            turn(4 * n + k)
+
+    loop(4, turns)
     loop(4, relay)
 
     low = iota((1, 128), 1) < 64
@@ -165,10 +178,6 @@
 
     loop(4, near_half)
 
-    def turn(i):
-        wt[i] = w0[i].T
-
-    loop(16, turn)
     load_ranks.wait()
     k_of = iota((64, 128), 0)
 

time: 40.6 us -> 40.3 us (level)
  no operation moved by 1% of the time
where the time goes in v7:
time: 40.3 us; the launch traced here: 40 us
  Pallas kernels  38.1 us (95%)
  local copies, waits for them, and re-layouts  1.31 us (3%)
  between operations  0.64 us (2%)
    pallas_call x1, Pallas kernels, on_device(): pl.pallas_call(kernel, out_shape=(pltpu.VMEM((8, 2, 8, 64), BF16), pltpu....  38.1 us

profile of v7, /device:TPU:1, one launch (start us, length us, event | category | flops | bytes accessed | tf_op | source)
XLA Modules:
  0.0 40.0 jit_solution(16511526760196601073)
XLA Ops:
  0.6 38.1 %shard_map.86 = (bf16[8,2,8,64]{3,2,1,0:T(8,128)(2,1)S(1)}, bf16[64,128]{1,0:T(8,128)(2,1)S(1)}) custom-call(f32[64,16,64]{2,1,0:T(8,128)} %right_ref.1, bf16[64,8,64]{2,1,0:T(8,128)(2,1)} %sol_ref.1, bf16[8,1024,512]{2,1,0:T(8,128)(2,1)} %basis_ref.1, bf16[8,64,16,64]{3,2,1,0:T(8,128)(2,1)} %wb_ref.1, s32[8,16]{1,0:T(8,128)} %ranks_ref.1, ...), custom_call_target="tpu_custom_call" | custom-call | flops 700000000 | bytes 12000000 | tf_op jit(solution)/shard_map/pallas_call | solution.py:329
  38.7 0.6 %copy.10 = bf16[64,16,8]{0,2,1:T(8,128)(2,1)} copy(bf16[64,16,8]{0,2,1:T(8,128)(2,1)S(1)} %bitcast.3) | data formatting | bytes 32768
  39.3 0.7 %reshape.11 = bf16[64,2,64]{2,1,0:T(2,128)(2,1)} reshape(bf16[64,128]{1,0:T(8,128)(2,1)S(1)} %get-tuple-element.5) | data formatting | bytes 32768 | tf_op jit(solution)/shard_map/reshape | solution.py:373

commit v8 on v7

--- a/solution.py
+++ b/solution.py
@@ -11,6 +11,7 @@
 I32 = jnp.int32
 N = 8
 NEAR = (2, 6, 1, 7)
+ROW_ORDER = (4, 5, 2, 3, 6, 7, 1)
 FAR_FIRST = (4, 3, 5, 2, 6, 1, 7)
 
 
@@ -74,6 +75,13 @@
         seven = ref.at[pl.ds(0, N - 1)]
         pltpu.make_async_copy(seven, seven, sem.at[0]).wait()
 
+    def row_at(k):
+        return lax.rem(r // 2 + k // 2, 4) * 2 + lax.rem(r + k % 2, 2)
+
+    def arrived(ref, sem, far):
+        some = ref.at[pl.ds(0, 2 if far else 5)]
+        pltpu.make_async_copy(some, some, sem.at[far]).wait()
+
     def away(n):
         return 4 + (n + 1) // 2 * (1 - 2 * lax.rem(n, 2))
 
@@ -200,15 +208,11 @@
         return jnp.where(low, sums[0], sums[1]) + swap(jnp.where(low, sums[1], sums[0]))
 
     def p2(d, to):
-        return remote(msg.at[d], part.at[d], p2_send, p2_recv, 0, "row", to)
-
-    def send_update(n):
-        d = away(n)
-        to = lax.rem(r + d, N)
-        msg[d] = update(to).astype(BF16)
-        p2(d, to).start()
-
-    loop(N - 1, send_update)
+        return remote(msg.at[d], part.at[d], p2_send, p2_recv, int(d // 2 == 2), "row", to)
+
+    for k in ROW_ORDER:
+        msg[k] = update(row_at(k)).astype(BF16)
+        p2(k, row_at(k)).start()
     own_update = update(r)
 
     load_map.wait()
@@ -249,9 +253,11 @@
         [right_f[pl.ds(base + h, 64, stride=8), :] for h in range(2)], axis=0).T
 
     acc = right_t - own_update
-    all_seven(part, p2_recv)
-    for d in range(1, N):
-        acc = acc - part[d].astype(F32)
+    for far in (0, 1):
+        arrived(part, p2_recv, far)
+        for k in ROW_ORDER:
+            if int(k // 2 == 2) == far:
+                acc = acc - part[k].astype(F32)
     red[...] = acc.astype(BF16)
     redg[c] = acc.astype(BF16)
 
@@ -285,12 +291,21 @@
     solg[r] = solved
 
     def p4(d, to):
-        return remote(solg.at[r], solg.at[r], p4_send, p4_recv, 0, "row", to)
-
-    loop(N - 1, lambda n: p4(away(n), lax.rem(r + away(n), N)).start())
-    all_seven(solg, p4_recv)
-
-    picked = dot(selm[...], solg[...].reshape(512, 128))
+        return remote(solg.at[r], solg.at[r], p4_send, p4_recv, int(d // 2 == 2), "row", to)
+
+    for k in ROW_ORDER:
+        p4(k, row_at(k)).start()
+
+    def picked_from(chips):
+        at = [lax.rem(r // 2 + k, 4) for k in chips]
+        table = jnp.concatenate([selm[:, pl.ds(pl.multiple_of(p * 128, 128), 128)] for p in at], axis=1)
+        rows = jnp.concatenate([solg[pl.ds(2 * p, 2)].reshape(128, 128) for p in at], axis=0)
+        return dot(table, rows)
+
+    arrived(solg, p4_recv, 0)
+    picked = picked_from((0, 1, 3))
+    arrived(solg, p4_recv, 1)
+    picked = picked + picked_from((2,))
     rows = jnp.where(low, picked[0:256], picked[256:512])
     rows = (rows + swap(rows)).reshape(8, 32, 128)
     pk[...] = jnp.where(low, rows[:, 0:16], rows[:, 16:32]).astype(BF16)
@@ -310,9 +325,10 @@
 
     loop(28, sent)
     all_seven(invg, inv_send)
-    all_seven(msg, p2_send)
+    for far in (0, 1):
+        arrived(msg, p2_send, far)
+        arrived(solg, p4_send, far)
     all_seven(redg, p3_send)
-    all_seven(solg, p4_send)
 
     all_seven(chg, p5_recv)
     got = chg[...].reshape(128, 128)
@@ -361,8 +377,8 @@
             pltpu.VMEM((8, 16, 128), BF16),
             dma((6,)), dma((8,)), dma((7, 4)), dma((7, 4)),
             dma((1,)), dma((1,)),
-            dma((1,)), dma((1,)), dma((1,)), dma((1,)),
-            dma((1,)), dma((1,)), dma((1,)), dma((1,)),
+            dma((2,)), dma((2,)), dma((1,)), dma((1,)),
+            dma((2,)), dma((2,)), dma((1,)), dma((1,)),
         ],
         compiler_params=pltpu.CompilerParams(
             collective_id=0, has_side_effects=True, vmem_limit_bytes=56 * 1024 * 1024

time: 40.3 us -> 40.2 us (level)
  no operation moved by 1% of the time
where the time goes in v8:
time: 40.2 us; the launch traced here: 40.1 us
  Pallas kernels  38.2 us (95%)
  local copies, waits for them, and re-layouts  1.31 us (3%)
  between operations  0.64 us (2%)
    pallas_call x1, Pallas kernels, on_device(): pl.pallas_call(kernel, out_shape=(pltpu.VMEM((8, 2, 8, 64), BF16), pltpu....  38.2 us

profile of v8, /device:TPU:1, one launch (start us, length us, event | category | flops | bytes accessed | tf_op | source)
XLA Modules:
  0.0 40.1 jit_solution(2644331374125865524)
XLA Ops:
  0.6 38.2 %shard_map.86 = (bf16[8,2,8,64]{3,2,1,0:T(8,128)(2,1)S(1)}, bf16[64,128]{1,0:T(8,128)(2,1)S(1)}) custom-call(f32[64,16,64]{2,1,0:T(8,128)} %right_ref.1, bf16[64,8,64]{2,1,0:T(8,128)(2,1)} %sol_ref.1, bf16[8,1024,512]{2,1,0:T(8,128)(2,1)} %basis_ref.1, bf16[8,64,16,64]{3,2,1,0:T(8,128)(2,1)} %wb_ref.1, s32[8,16]{1,0:T(8,128)} %ranks_ref.1, ...), custom_call_target="tpu_custom_call" | custom-call | flops 700000000 | bytes 12000000 | tf_op jit(solution)/shard_map/pallas_call | solution.py:345
  38.8 0.6 %copy.10 = bf16[64,16,8]{0,2,1:T(8,128)(2,1)} copy(bf16[64,16,8]{0,2,1:T(8,128)(2,1)S(1)} %bitcast.3) | data formatting | bytes 32768
  39.4 0.7 %reshape.11 = bf16[64,2,64]{2,1,0:T(2,128)(2,1)} reshape(bf16[64,128]{1,0:T(8,128)(2,1)S(1)} %get-tuple-element.5) | data formatting | bytes 32768 | tf_op jit(solution)/shard_map/reshape | solution.py:389

commit v9 on v8

--- a/solution.py
+++ b/solution.py
@@ -262,9 +262,10 @@
     redg[c] = acc.astype(BF16)
 
     def p3(d, to):
-        return remote(red, redg.at[c], p3_send, p3_recv, 0, "col", to)
-
-    loop(N - 1, lambda n: p3(away(n), lax.rem(c + away(n), N)).start())
+        return remote(red, redg.at[c], p3_send, p3_recv, int(d in (3, 4, 5)), "col", to)
+
+    for d in FAR_FIRST:
+        p3(d, lax.rem(c + d, N)).start()
     load_inv.wait()
     all_seven(invg, inv_recv)
     for h in range(2):
@@ -284,9 +285,14 @@
     for h in range(2):
         s5[h] = jnp.where((qb == found) & ((rank_i >> 4) == h), 1.0, 0.0).astype(BF16)
 
-    all_seven(redg, p3_recv)
-
-    s = dot(invl[...], redg[...].reshape(512, 128))
+
+    s = 0.0
+    for far in (0, 1):
+        some = redg.at[pl.ds(0, 3 if far else 4)]
+        pltpu.make_async_copy(some, some, p3_recv.at[far]).wait()
+        at = [lax.rem(near + 2 * far + k, 4) for k in range(2)]
+        tiles = jnp.concatenate([invl[:, pl.ds(pl.multiple_of(p * 128, 128), 128)] for p in at], axis=1)
+        s = s + dot(tiles, jnp.concatenate([redg[pl.ds(2 * p, 2)].reshape(128, 128) for p in at], axis=0))
     solved = jnp.where(low, s[0:64], s[64:128]).astype(BF16)
     solg[r] = solved
 
@@ -328,7 +334,9 @@
     for far in (0, 1):
         arrived(msg, p2_send, far)
         arrived(solg, p4_send, far)
-    all_seven(redg, p3_send)
+    for far in (0, 1):
+        some = redg.at[pl.ds(0, 3 if far else 4)]
+        pltpu.make_async_copy(some, some, p3_send.at[far]).wait()
 
     all_seven(chg, p5_recv)
     got = chg[...].reshape(128, 128)
@@ -377,7 +385,7 @@
             pltpu.VMEM((8, 16, 128), BF16),
             dma((6,)), dma((8,)), dma((7, 4)), dma((7, 4)),
             dma((1,)), dma((1,)),
-            dma((2,)), dma((2,)), dma((1,)), dma((1,)),
+            dma((2,)), dma((2,)), dma((2,)), dma((2,)),
             dma((2,)), dma((2,)), dma((1,)), dma((1,)),
         ],
         compiler_params=pltpu.CompilerParams(

time: 40.2 us -> 40.1 us (level)
  no operation moved by 1% of the time
where the time goes in v9:
time: 40.1 us; the launch traced here: 40 us
  Pallas kernels  38 us (95%)
  local copies, waits for them, and re-layouts  1.31 us (3%)
  between operations  0.64 us (2%)
    pallas_call x1, Pallas kernels, on_device(): pl.pallas_call(kernel, out_shape=(pltpu.VMEM((8, 2, 8, 64), BF16), pltpu....  38 us

profile of v9, /device:TPU:1, one launch (start us, length us, event | category | flops | bytes accessed | tf_op | source)
XLA Modules:
  0.0 40.0 jit_solution(10367880309778027084)
XLA Ops:
  0.6 38.0 %shard_map.86 = (bf16[8,2,8,64]{3,2,1,0:T(8,128)(2,1)S(1)}, bf16[64,128]{1,0:T(8,128)(2,1)S(1)}) custom-call(f32[64,16,64]{2,1,0:T(8,128)} %right_ref.1, bf16[64,8,64]{2,1,0:T(8,128)(2,1)} %sol_ref.1, bf16[8,1024,512]{2,1,0:T(8,128)(2,1)} %basis_ref.1, bf16[8,64,16,64]{3,2,1,0:T(8,128)(2,1)} %wb_ref.1, s32[8,16]{1,0:T(8,128)} %ranks_ref.1, ...), custom_call_target="tpu_custom_call" | custom-call | flops 700000000 | bytes 12000000 | tf_op jit(solution)/shard_map/pallas_call | solution.py:353
  38.7 0.6 %copy.10 = bf16[64,16,8]{0,2,1:T(8,128)(2,1)} copy(bf16[64,16,8]{0,2,1:T(8,128)(2,1)S(1)} %bitcast.3) | data formatting | bytes 32768
  39.3 0.7 %reshape.11 = bf16[64,2,64]{2,1,0:T(2,128)(2,1)} reshape(bf16[64,128]{1,0:T(8,128)(2,1)S(1)} %get-tuple-element.5) | data formatting | bytes 32768 | tf_op jit(solution)/shard_map/reshape | solution.py:397

commit v10 on v9

--- a/solution.py
+++ b/solution.py
@@ -214,6 +214,31 @@
         msg[k] = update(row_at(k)).astype(BF16)
         p2(k, row_at(k)).start()
     own_update = update(r)
+
+    load_right.wait()
+    right_f[...] = right_v[...].reshape(512, 64)
+    base = 2 * lax.rem(r, 4)
+    right_t = jnp.concatenate(
+        [right_f[pl.ds(base + h, 64, stride=8), :] for h in range(2)], axis=0).T
+
+    acc = right_t - own_update
+    for far in (0, 1):
+        arrived(part, p2_recv, far)
+        for k in ROW_ORDER:
+            if int(k // 2 == 2) == far:
+                acc = acc - part[k].astype(F32)
+    red[...] = acc.astype(BF16)
+    redg[c] = acc.astype(BF16)
+
+    def p3(d, to):
+        return remote(red, redg.at[c], p3_send, p3_recv, int(d in (3, 4, 5)), "col", to)
+
+    for d in FAR_FIRST:
+        p3(d, lax.rem(c + d, N)).start()
+    load_inv.wait()
+    all_seven(invg, inv_recv)
+    for h in range(2):
+        invl[h * 64:(h + 1) * 64, :] = invg[:, h].astype(F32).reshape(64, 512).astype(BF16)
 
     load_map.wait()
     w = map_v[...]
@@ -245,31 +270,6 @@
     ra, la = iota((64, 512), 0), iota((64, 512), 1)
     selm[512:576, :] = jnp.where(
         la == ((ra >> 3) << 6) + r * 8 + (ra & 7), 1.0, 0.0).astype(BF16)
-
-    load_right.wait()
-    right_f[...] = right_v[...].reshape(512, 64)
-    base = 2 * lax.rem(r, 4)
-    right_t = jnp.concatenate(
-        [right_f[pl.ds(base + h, 64, stride=8), :] for h in range(2)], axis=0).T
-
-    acc = right_t - own_update
-    for far in (0, 1):
-        arrived(part, p2_recv, far)
-        for k in ROW_ORDER:
-            if int(k // 2 == 2) == far:
-                acc = acc - part[k].astype(F32)
-    red[...] = acc.astype(BF16)
-    redg[c] = acc.astype(BF16)
-
-    def p3(d, to):
-        return remote(red, redg.at[c], p3_send, p3_recv, int(d in (3, 4, 5)), "col", to)
-
-    for d in FAR_FIRST:
-        p3(d, lax.rem(c + d, N)).start()
-    load_inv.wait()
-    all_seven(invg, inv_recv)
-    for h in range(2):
-        invl[h * 64:(h + 1) * 64, :] = invg[:, h].astype(F32).reshape(64, 512).astype(BF16)
 
     x = map_v[:, pl.ds(pl.multiple_of((c // 2) * 128, 128), 128)]
     x_swapped = swap(x)

time: 40.1 us -> 40.2 us (level)
  no operation moved by 1% of the time
where the time goes in v10:
time: 40.2 us; the launch traced here: 40.1 us
  Pallas kernels  38.1 us (95%)
  local copies, waits for them, and re-layouts  1.31 us (3%)
  between operations  0.64 us (2%)
    pallas_call x1, Pallas kernels, on_device(): pl.pallas_call(kernel, out_shape=(pltpu.VMEM((8, 2, 8, 64), BF16), pltpu....  38.1 us

profile of v10, /device:TPU:1, one launch (start us, length us, event | category | flops | bytes accessed | tf_op | source)
XLA Modules:
  0.0 40.1 jit_solution(12074854275822142575)
XLA Ops:
  0.6 38.1 %shard_map.86 = (bf16[8,2,8,64]{3,2,1,0:T(8,128)(2,1)S(1)}, bf16[64,128]{1,0:T(8,128)(2,1)S(1)}) custom-call(f32[64,16,64]{2,1,0:T(8,128)} %right_ref.1, bf16[64,8,64]{2,1,0:T(8,128)(2,1)} %sol_ref.1, bf16[8,1024,512]{2,1,0:T(8,128)(2,1)} %basis_ref.1, bf16[8,64,16,64]{3,2,1,0:T(8,128)(2,1)} %wb_ref.1, s32[8,16]{1,0:T(8,128)} %ranks_ref.1, ...), custom_call_target="tpu_custom_call" | custom-call | flops 700000000 | bytes 12000000 | tf_op jit(solution)/shard_map/pallas_call | solution.py:353
  38.8 0.6 %copy.10 = bf16[64,16,8]{0,2,1:T(8,128)(2,1)} copy(bf16[64,16,8]{0,2,1:T(8,128)(2,1)S(1)} %bitcast.3) | data formatting | bytes 32768
  39.4 0.7 %reshape.11 = bf16[64,2,64]{2,1,0:T(2,128)(2,1)} reshape(bf16[64,128]{1,0:T(8,128)(2,1)S(1)} %get-tuple-element.5) | data formatting | bytes 32768 | tf_op jit(solution)/shard_map/reshape | solution.py:397
